TPU v7x, 32 devices: a whole 2x2x4 slice. The times are simulated.
32 devices in a mesh: dp: 8 (over y, x, core), mp: 4 (over z).
Axes of the slice: x: 2, y: 2, z: 4, core: 2. Of those that a mesh axis runs over, the one named last changes fastest.
Arguments:
- block_input: bfloat16 [2, 8, 256, 1536], P(None, 'dp', 'mp'), may hold values from -6 to 6
- out_grad: bfloat16 [2, 8, 256, 1536], P(None, 'dp', 'mp'), may hold values from -6 to 6
- doc_lengths: int32 [2, 8, 4], P(None, 'dp'), may hold values from 1 to 224, 256 in all within a row
- attn_gain: bfloat16 [1536], P('dp'), may hold values from 0.5 to 1.5
- qkv_weight: bfloat16 [3, 1536, 1536], P(None, 'dp', 'mp'), may hold values from -0.15625 to 0.15625
- conv_kernel: float32 [16, 6, 11], P('mp'), may hold values from -0.25 to 1.25
- head_mixing: float32 [8, 2, 2], P('mp'), may hold values from -0.5 to 1.5
- group_gain: bfloat16 [1536], P('mp'), may hold values from 0.25 to 1.75
- out_weight: bfloat16 [1536, 1536], P('mp', 'dp'), may hold values from -0.15625 to 0.15625
- mlp_gain: bfloat16 [1536], P('dp'), may hold values from 0.5 to 1.5
- gate_weight: bfloat16 [1536, 4096], P('dp', 'mp'), may hold values from -0.15625 to 0.15625
- up_weight: bfloat16 [1536, 4096], P('dp', 'mp'), may hold values from -0.15625 to 0.15625
- down_weight: bfloat16 [4096, 1536], P('mp', 'dp'), may hold values from -0.09375 to 0.09375
Outputs:
- block_output: bfloat16 [2, 8, 256, 1536], P(None, 'dp', 'mp')
- input_grad: float32 [2, 8, 256, 1536], P(None, 'dp', 'mp')
- attn_gain_grad: float32 [1536], P('dp')
- qkv_grad: float32 [3, 1536, 1536], P(None, 'dp', 'mp')
- kernel_grad: float32 [16, 6, 11], P('mp')
- mixing_grad: float32 [8, 2, 2], P('mp')
- group_gain_grad: float32 [1536], P('mp')
- out_weight_grad: float32 [1536, 1536], P('mp', 'dp')
- mlp_gain_grad: float32 [1536], P('dp')
- gate_grad: float32 [1536, 4096], P('dp', 'mp')
- up_grad: float32 [1536, 4096], P('dp', 'mp')
- down_grad: float32 [4096, 1536], P('mp', 'dp')
Inputs may be any that keep to these rules, and one draw needn't show every extreme that they name: `doc_lengths`: each group's 4 lengths sum to 256; the longest is 224.
All inputs are finite; a program needn't handle non-finite values.
Results may differ from a plain program's by a relative error of at most 0.023.
Values may be sent and summed in bfloat16 or wider, within the bound.
No kernel may reach another device: no remote copies, remote signals or barrier semaphores. Data moves between devices by JAX's collectives and lax.ppermute only.
A program may use at most 192 MiB of HBM per device.

v0:
```python
import math

import jax
import jax.numpy as jnp
from jax import lax
from jax.sharding import PartitionSpec as P

CQ = 6
CK = 11


EPS = 1e-05


def segment_ids(lengths, length):
    ends = jnp.cumsum(lengths)
    places = jnp.arange(length, dtype=jnp.int32)
    return jnp.sum((places[:, None] >= ends[None, :]).astype(jnp.int32), axis=1)


def allowed(segment):
    places = jnp.arange(segment.shape[0], dtype=jnp.int32)
    return (places[None, :] <= places[:, None]) & (segment[None, :] == segment[:, None])


def conv_forward(zeroed, kernel, segment):
    length = zeroed.shape[1]
    center = CK // 2
    padded = jnp.pad(zeroed, ((0, 0), (CQ - 1, 0), (center, CK - 1 - center)))
    seg_pad = jnp.pad(segment, (CQ - 1, 0), constant_values=-1)
    summed = jnp.zeros_like(zeroed)
    for query_shift in range(CQ):
        earlier_rows = padded[:, CQ - 1 - query_shift : CQ - 1 - query_shift + length, :]
        same_doc = (
            seg_pad[CQ - 1 - query_shift : CQ - 1 - query_shift + length] == segment
        ).astype(jnp.float32)
        partial_sum = jnp.zeros_like(zeroed)
        for key_shift in range(CK):
            partial_sum = (
                partial_sum
                + kernel[:, query_shift, key_shift][:, None, None]
                * earlier_rows[:, :, CK - 1 - key_shift : CK - 1 - key_shift + length]
            )
        summed = summed + same_doc[None, :, None] * partial_sum
    return summed


def conv_backward(grad_logits, zeroed, kernel, segment):
    length = grad_logits.shape[1]
    center = CK // 2
    padded = jnp.pad(zeroed, ((0, 0), (CQ - 1, 0), (center, CK - 1 - center)))
    seg_pad = jnp.pad(segment, (CQ - 1, 0), constant_values=-1)
    grad_zeroed = jnp.zeros_like(grad_logits)
    kernel_rows = []
    for query_shift in range(CQ):
        same_doc = (
            seg_pad[CQ - 1 - query_shift : CQ - 1 - query_shift + length] == segment
        ).astype(jnp.float32)
        weighted = grad_logits * same_doc[None, :, None]
        earlier_rows = padded[:, CQ - 1 - query_shift : CQ - 1 - query_shift + length, :]
        later_rows = jnp.pad(weighted, ((0, 0), (0, CQ - 1), (center, CK - 1 - center)))[
            :, query_shift : query_shift + length, :
        ]
        partial_sum = jnp.zeros_like(grad_logits)
        taps = []
        for key_shift in range(CK):
            taps.append(
                jnp.sum(
                    weighted * earlier_rows[:, :, CK - 1 - key_shift : CK - 1 - key_shift + length],
                    axis=(1, 2),
                )
            )
            partial_sum = (
                partial_sum
                + kernel[:, query_shift, key_shift][:, None, None]
                * later_rows[:, :, key_shift : key_shift + length]
            )
        grad_zeroed = grad_zeroed + partial_sum
        kernel_rows.append(jnp.stack(taps, axis=1))
    return (grad_zeroed, jnp.stack(kernel_rows, axis=1))


def attention_logits(query, keys, kernel, segment, mask, scale_factor):
    scores = (
        jnp.einsum("thd,shd->hts", query, keys, preferred_element_type=jnp.float32) * scale_factor
    )
    zeroed = jnp.where(mask[None], scores, 0.0)
    logits = conv_forward(zeroed, kernel, segment)
    return (zeroed, jnp.where(mask[None], logits, -jnp.inf))


def rms_forward(values):
    scale = lax.rsqrt(jnp.mean(values * values, axis=-1, keepdims=True) + EPS)
    return (values * scale, scale)


def rms_backward(grad_normed, normalized, scale, gain):
    upstream = grad_normed * gain
    grad_values = scale * (
        upstream - normalized * jnp.mean(upstream * normalized, axis=-1, keepdims=True)
    )
    return (grad_values, jnp.sum(grad_normed * normalized, axis=0))


def shards(
    block_input,
    out_grad,
    doc_lengths,
    attn_gain,
    qkv_weight,
    conv_kernel,
    head_mixing,
    group_gain,
    out_weight,
    mlp_gain,
    gate_weight,
    up_weight,
    down_weight,
):
    batches = block_input.shape[0]
    shard_rows = block_input.shape[2]
    length = shard_rows * lax.axis_size("mp")
    local_heads = conv_kernel.shape[0]
    head_size = qkv_weight.shape[2] // local_heads
    scale_factor = 1.0 / math.sqrt(head_size)
    group_gain_f = group_gain.astype(jnp.float32)
    grad_totals = None
    head_totals = None
    outputs = []
    input_grads = []
    for batch in range(batches):
        gathered = (
            lax.all_gather(attn_gain, "dp", axis=0, tiled=True),
            lax.all_gather(qkv_weight, "dp", axis=1, tiled=True),
            lax.all_gather(out_weight, "dp", axis=1, tiled=True),
            lax.all_gather(mlp_gain, "dp", axis=0, tiled=True),
            lax.all_gather(gate_weight, "dp", axis=0, tiled=True),
            lax.all_gather(up_weight, "dp", axis=0, tiled=True),
            lax.all_gather(down_weight, "dp", axis=1, tiled=True),
        )
        full_attn_gain, full_qkv, full_out, full_mlp_gain, full_gate, full_up, full_down = gathered
        gain_first = full_attn_gain.astype(jnp.float32)
        gain_second = full_mlp_gain.astype(jnp.float32)
        segment = segment_ids(doc_lengths[batch, 0], length)
        mask = allowed(segment)
        tokens_in = block_input[batch, 0].astype(jnp.float32)
        normal_first, scale_first = rms_forward(tokens_in)
        normed_in = (normal_first * gain_first).astype(jnp.bfloat16)
        all_normed = lax.all_gather(normed_in, "mp", axis=0, tiled=True)
        projected = jnp.einsum(
            "td,cde->cte", all_normed, full_qkv, preferred_element_type=jnp.float32
        ).astype(jnp.bfloat16)
        query = projected[0].reshape(length, local_heads, head_size)
        keys = projected[1].reshape(length, local_heads, head_size)
        values = projected[2].reshape(length, local_heads, head_size)
        zeroed, masked = attention_logits(query, keys, conv_kernel, segment, mask, scale_factor)
        top = jnp.max(masked, axis=-1, keepdims=True)
        log_total = top + jnp.log(jnp.sum(jnp.exp(masked - top), axis=-1, keepdims=True))
        probs = jnp.exp(masked - log_total)
        pairs = probs.reshape(local_heads // 2, 2, length, length)
        mixed = jnp.sum(head_mixing[:, :, :, None, None] * pairs[:, None, :, :, :], axis=2)
        mixed = mixed.reshape(local_heads, length, length).astype(jnp.bfloat16)
        heads_out = jnp.einsum("hts,shd->thd", mixed, values, preferred_element_type=jnp.float32)
        centered = heads_out - jnp.mean(heads_out, axis=-1, keepdims=True)
        inv_std = lax.rsqrt(jnp.mean(centered * centered, axis=-1, keepdims=True) + EPS)
        normed_heads = centered * inv_std
        flat_heads = normed_heads.reshape(length, local_heads * head_size)
        grouped = (flat_heads * group_gain_f).astype(jnp.bfloat16)
        attended = lax.psum_scatter(
            jnp.dot(grouped, full_out, preferred_element_type=jnp.float32).astype(jnp.bfloat16),
            "mp",
            scatter_dimension=0,
            tiled=True,
        ).astype(jnp.float32)
        hidden_in = tokens_in + attended
        normal_second, scale_second = rms_forward(hidden_in)
        normed_mid = (normal_second * gain_second).astype(jnp.bfloat16)
        all_mid = lax.all_gather(normed_mid, "mp", axis=0, tiled=True)
        gate = jnp.dot(all_mid, full_gate, preferred_element_type=jnp.float32)
        upward = jnp.dot(all_mid, full_up, preferred_element_type=jnp.float32)
        sigmoid_gate = jax.nn.sigmoid(gate)
        swish = gate * sigmoid_gate
        hidden = (swish * upward).astype(jnp.bfloat16)
        mlp_out = lax.psum_scatter(
            jnp.dot(hidden, full_down, preferred_element_type=jnp.float32).astype(jnp.bfloat16),
            "mp",
            scatter_dimension=0,
            tiled=True,
        ).astype(jnp.float32)
        outputs.append((hidden_in + mlp_out).astype(jnp.bfloat16))
        grad_rows = out_grad[batch, 0]
        all_grad = lax.all_gather(grad_rows, "mp", axis=0, tiled=True)
        grad_hidden = jnp.dot(all_grad, full_down.T, preferred_element_type=jnp.float32)
        grad_down = jnp.dot(hidden.T, all_grad, preferred_element_type=jnp.float32)
        grad_gate = (
            grad_hidden * upward * sigmoid_gate * (1.0 + gate * (1.0 - sigmoid_gate))
        ).astype(jnp.bfloat16)
        grad_up = (grad_hidden * swish).astype(jnp.bfloat16)
        grad_gate_w = jnp.dot(all_mid.T, grad_gate, preferred_element_type=jnp.float32)
        grad_up_w = jnp.dot(all_mid.T, grad_up, preferred_element_type=jnp.float32)
        grad_mid = lax.psum_scatter(
            (
                jnp.dot(grad_gate, full_gate.T, preferred_element_type=jnp.float32)
                + jnp.dot(grad_up, full_up.T, preferred_element_type=jnp.float32)
            ).astype(jnp.bfloat16),
            "mp",
            scatter_dimension=0,
            tiled=True,
        ).astype(jnp.float32)
        grad_from_mid, mlp_gain_part = rms_backward(
            grad_mid, normal_second, scale_second, gain_second
        )
        grad_hidden_in = grad_rows.astype(jnp.float32) + grad_from_mid
        all_attn_grad = lax.all_gather(
            grad_hidden_in.astype(jnp.bfloat16), "mp", axis=0, tiled=True
        )
        grad_grouped = jnp.dot(all_attn_grad, full_out.T, preferred_element_type=jnp.float32)
        grad_out_w = jnp.dot(grouped.T, all_attn_grad, preferred_element_type=jnp.float32)
        group_gain_part = jnp.sum(grad_grouped * flat_heads, axis=0)
        grad_normed = (grad_grouped * group_gain_f).reshape(length, local_heads, head_size)
        grad_heads = inv_std * (
            grad_normed
            - jnp.mean(grad_normed, axis=-1, keepdims=True)
            - normed_heads * jnp.mean(grad_normed * normed_heads, axis=-1, keepdims=True)
        )
        grad_heads = grad_heads.astype(jnp.bfloat16)
        zeroed_again, masked_again = attention_logits(
            query, keys, conv_kernel, segment, mask, scale_factor
        )
        probs_again = jnp.exp(masked_again - log_total)
        pairs_again = probs_again.reshape(local_heads // 2, 2, length, length)
        grad_mixed = jnp.einsum(
            "thd,shd->hts", grad_heads, values, preferred_element_type=jnp.float32
        )
        grad_values = jnp.einsum(
            "hts,thd->shd", mixed, grad_heads, preferred_element_type=jnp.float32
        )
        grad_pairs = grad_mixed.reshape(local_heads // 2, 2, length, length)
        mixing_part = jnp.einsum(
            "gaij,gbij->gab", grad_pairs, pairs_again, precision=lax.Precision.HIGHEST
        )
        grad_probs = jnp.sum(
            head_mixing[:, :, :, None, None] * grad_pairs[:, :, None, :, :], axis=1
        )
        grad_probs = grad_probs.reshape(local_heads, length, length)
        grad_logits = probs_again * (
            grad_probs - jnp.sum(grad_probs * probs_again, axis=-1, keepdims=True)
        )
        grad_zeroed, kernel_part = conv_backward(grad_logits, zeroed_again, conv_kernel, segment)
        grad_scores = jnp.where(mask[None], grad_zeroed, 0.0).astype(jnp.bfloat16)
        grad_query = (
            jnp.einsum("hts,shd->thd", grad_scores, keys, preferred_element_type=jnp.float32)
            * scale_factor
        ).astype(jnp.bfloat16)
        grad_keys = (
            jnp.einsum("hts,thd->shd", grad_scores, query, preferred_element_type=jnp.float32)
            * scale_factor
        ).astype(jnp.bfloat16)
        grad_proj = jnp.stack([grad_query, grad_keys, grad_values.astype(jnp.bfloat16)]).reshape(
            3, length, local_heads * head_size
        )
        grad_qkv_w = jnp.einsum(
            "td,cte->cde", all_normed, grad_proj, preferred_element_type=jnp.float32
        )
        grad_in = lax.psum_scatter(
            jnp.einsum(
                "cte,cde->td", grad_proj, full_qkv, preferred_element_type=jnp.float32
            ).astype(jnp.bfloat16),
            "mp",
            scatter_dimension=0,
            tiled=True,
        ).astype(jnp.float32)
        grad_from_in, attn_gain_part = rms_backward(grad_in, normal_first, scale_first, gain_first)
        input_grads.append(grad_hidden_in + grad_from_in)
        local_grads = (
            attn_gain_part,
            grad_qkv_w,
            grad_out_w,
            mlp_gain_part,
            grad_gate_w,
            grad_up_w,
            grad_down,
        )
        head_local = (kernel_part, mixing_part, group_gain_part)
        head_totals = (
            head_local if head_totals is None else jax.tree.map(jnp.add, head_totals, head_local)
        )
        shares = (
            lax.psum_scatter(local_grads[0], "dp", scatter_dimension=0, tiled=True),
            lax.psum_scatter(local_grads[1], "dp", scatter_dimension=1, tiled=True),
            lax.psum_scatter(local_grads[2], "dp", scatter_dimension=1, tiled=True),
            lax.psum_scatter(local_grads[3], "dp", scatter_dimension=0, tiled=True),
            lax.psum_scatter(local_grads[4], "dp", scatter_dimension=0, tiled=True),
            lax.psum_scatter(local_grads[5], "dp", scatter_dimension=0, tiled=True),
            lax.psum_scatter(local_grads[6], "dp", scatter_dimension=1, tiled=True),
        )
        grad_totals = shares if grad_totals is None else jax.tree.map(jnp.add, grad_totals, shares)
    attn_gain_grad, mlp_gain_grad = lax.psum((grad_totals[0], grad_totals[3]), "mp")
    kernel_grad, mixing_grad, group_gain_grad = lax.psum(
        (head_totals[0], head_totals[1], head_totals[2]), "dp"
    )
    block_output = jnp.stack(outputs)[:, None]
    input_grad = jnp.stack(input_grads)[:, None]
    return (
        block_output,
        input_grad,
        attn_gain_grad,
        grad_totals[1],
        kernel_grad,
        mixing_grad,
        group_gain_grad,
        grad_totals[2],
        mlp_gain_grad,
        grad_totals[4],
        grad_totals[5],
        grad_totals[6],
    )


def solution(mesh):
    return jax.shard_map(
        shards,
        mesh=mesh,
        in_specs=(
            P(None, "dp", "mp", None),
            P(None, "dp", "mp", None),
            P(None, "dp", None),
            P("dp"),
            P(None, "dp", "mp"),
            P("mp", None, None),
            P("mp", None, None),
            P("mp"),
            P("mp", "dp"),
            P("dp"),
            P("dp", "mp"),
            P("dp", "mp"),
            P("mp", "dp"),
        ),
        out_specs=(
            P(None, "dp", "mp", None),
            P(None, "dp", "mp", None),
            P("dp"),
            P(None, "dp", "mp"),
            P("mp", None, None),
            P("mp", None, None),
            P("mp"),
            P("mp", "dp"),
            P("dp"),
            P("dp", "mp"),
            P("dp", "mp"),
            P("mp", "dp"),
        ),
        check_vma=False,
    )
```

profile of v0, /device:TPU:0, one launch (start us, length us, event | category | flops | bytes accessed | tf_op | source)
XLA Modules:
  0.0 972.1 jit_solution(17576320882922973017)
XLA Ops:
  26.2 16.3 %all-reduce.22 = (bf16[1536]{0:T(1024)(128)(2,1)S(1)}, bf16[1536]{0:T(1024)(128)(2,1)}) all-reduce(bf16[1536]{0:T(1024)(128)(2,1)S(1)} %dynamic-update-slice, bf16[1536]{0:T(1024)(128)(2,1)S(1)} %dynamic-update-slice.1), channel_id=1, replica_groups=mesh['dp'=8,'mp'=4] {'dp'}, use_global_device_ids=true, to_apply=%add.16 | all-reduce | flops 3072 | bytes 12288
  42.7 18.3 %all_gather.53 = bf16[256,1536]{1,0:T(8,128)(2,1)S(1)} all-gather(bf16[64,1536]{1,0:T(8,128)(2,1)S(1)} %get-tuple-element.324), channel_id=1, replica_groups=mesh['dp'=8,'mp'=4] {'mp'}, dimensions={0}, use_global_device_ids=true | all-gather | bytes 983040 | tf_op jit(solution)/shard_map/all_gather | solution.py:149
  61.0 17.4 %all_gather.61 = bf16[256,1536]{1,0:T(8,128)(2,1)S(1)} all-gather(bf16[64,1536]{1,0:T(8,128)(2,1)S(1)} %get-tuple-element.325), channel_id=1, replica_groups=mesh['dp'=8,'mp'=4] {'mp'}, dimensions={0}, use_global_device_ids=true | all-gather | bytes 983040 | tf_op jit(solution)/shard_map/all_gather | solution.py:149
  90.0 19.7 %fusion.349 = (f32[4,256]{1,0:T(4,128)S(1)}, f32[4,256,256]{2,1,0:T(8,128)S(1)}) fusion(f32[4]{0:T(128)} %get-tuple-element.276, f32[4]{0:T(128)} %get-tuple-element.277, f32[4]{0:T(128)S(1)} %copy-done.101, f32[4]{0:T(128)S(1)} %copy-done.102, f32[4]{0:T(128)S(1)} %copy-done.103, f32[4]{0:T(128)S(1)} %copy-done.104, f32[4]{0:T(128)S(1)} %copy-done.105, ...), kind=kLoop, calls=%fused_computation.961 | loop fusion | flops 36174848 | bytes 2172960 | tf_op jit(solution)/shard_map/reduce_max | solution.py:157
  111.5 22.0 %fusion.348 = (f32[4,256]{1,0:T(4,128)}, f32[4,256,256]{2,1,0:T(8,128)}) fusion(f32[4]{0:T(128)} %get-tuple-element.276, f32[4]{0:T(128)} %get-tuple-element.277, f32[4]{0:T(128)} %get-tuple-element.213, f32[4]{0:T(128)} %get-tuple-element.214, f32[4]{0:T(128)} %get-tuple-element.215, f32[4]{0:T(128)} %get-tuple-element.216, f32[4]{0:T(128)} %get-tuple-element.217, ...), kind=kLoop, calls=%fused_computation.960 | loop fusion | flops 36174848 | bytes 2172960 | tf_op jit(solution)/shard_map/reduce_max | solution.py:157
  152.8 25.7 %all-gather.1 = bf16[1,1,256,1536]{3,2,1,0:T(8,128)(2,1)} all-gather(bf16[1,1,64,1536]{3,2,1,0:T(8,128)(2,1)S(1)} %get-tuple-element.330), channel_id=3, replica_groups=mesh['dp'=8,'mp'=4] {'mp'}, dimensions={2}, use_global_device_ids=true | all-gather | bytes 983040 | tf_op jit(solution)/shard_map/all_gather | solution.py:192
  178.5 24.1 %all-gather = bf16[1,1,256,1536]{3,2,1,0:T(8,128)(2,1)} all-gather(bf16[1,1,64,1536]{3,2,1,0:T(8,128)(2,1)S(1)} %get-tuple-element.331), channel_id=2, replica_groups=mesh['dp'=8,'mp'=4] {'mp'}, dimensions={2}, use_global_device_ids=true | all-gather | bytes 983040 | tf_op jit(solution)/shard_map/all_gather | solution.py:192
  208.1 19.0 %all_gather.57 = bf16[256,1536]{1,0:T(8,128)(2,1)S(1)} all-gather(bf16[64,1536]{1,0:T(8,128)(2,1)S(1)} %get-tuple-element.322), channel_id=1, replica_groups=mesh['dp'=8,'mp'=4] {'mp'}, dimensions={0}, use_global_device_ids=true | all-gather | bytes 983040 | tf_op jit(solution)/shard_map/all_gather | solution.py:178
  227.1 18.1 %all_gather.62 = bf16[256,1536]{1,0:T(8,128)(2,1)} all-gather(bf16[64,1536]{1,0:T(8,128)(2,1)S(1)} %get-tuple-element.323), channel_id=1, replica_groups=mesh['dp'=8,'mp'=4] {'mp'}, dimensions={0}, use_global_device_ids=true | all-gather | bytes 983040 | tf_op jit(solution)/shard_map/all_gather | solution.py:178
  245.2 3.9 fusion.357
  249.0 26.5 %all-gather.12.cloned.1.call-done = bf16[1536,1024]{1,0:T(8,128)(2,1)} async-done(((bf16[192,1024]{1,0:T(8,128)(2,1)}), bf16[1536,1024]{1,0:T(8,128)(2,1)}) %all-gather.12.cloned.1.call-update) | async-done | bytes 3145744 | tf_op jit(solution)/shard_map/all_gather | solution.py:137
  275.5 3.9 fusion.356
  279.4 30.4 %all-gather.16.cloned.1.call-done = bf16[1024,1536]{0,1:T(8,128)(2,1)} async-done(((bf16[1024,192]{0,1:T(8,128)(2,1)}), bf16[1024,1536]{0,1:T(8,128)(2,1)}) %all-gather.16.cloned.1.call-update) | async-done | bytes 3145744 | tf_op jit(solution)/shard_map/all_gather | solution.py:139
  309.7 5.0 multiply_convert_fusion.2
  330.8 4.0 convolution_convert_fusion
  334.9 7.6 reduce-scatter.24.cloned.1.call-done
  342.4 25.4 %reduce-scatter.28.cloned.1.call-done = bf16[64,1536]{1,0:T(8,128)(2,1)} async-done(((bf16[256,1536]{1,0:T(8,128)(2,1)}), bf16[64,1536]{1,0:T(8,128)(2,1)}) %reduce-scatter.28.cloned.1.call-update) | async-done | bytes 196624 | tf_op jit(solution)/shard_map/reduce_scatter | solution.py:201
  369.8 23.3 %reduce-scatter.22.cloned.1.call-done = bf16[64,1536]{1,0:T(8,128)(2,1)} async-done(((bf16[256,1536]{1,0:T(8,128)(2,1)}), bf16[64,1536]{1,0:T(8,128)(2,1)}) %reduce-scatter.22.cloned.1.call-update) | async-done | bytes 196624 | tf_op jit(solution)/shard_map/reduce_scatter | solution.py:184
  395.6 18.0 %all_gather.64 = bf16[256,1536]{1,0:T(8,128)(2,1)S(1)} all-gather(bf16[64,1536]{1,0:T(8,128)(2,1)S(1)} %get-tuple-element.311), channel_id=1, replica_groups=mesh['dp'=8,'mp'=4] {'mp'}, dimensions={0}, use_global_device_ids=true | all-gather | bytes 983040 | tf_op jit(solution)/shard_map/all_gather | solution.py:214
  415.7 17.6 %all_gather.66 = bf16[256,1536]{1,0:T(8,128)(2,1)S(1)} all-gather(bf16[64,1536]{1,0:T(8,128)(2,1)S(1)} %get-tuple-element.312), channel_id=1, replica_groups=mesh['dp'=8,'mp'=4] {'mp'}, dimensions={0}, use_global_device_ids=true | all-gather | bytes 983040 | tf_op jit(solution)/shard_map/all_gather | solution.py:214
  445.8 6.2 multiply_reduce_fusion.4
  452.0 4.4 multiply_reduce_fusion.15
  456.4 4.4 multiply_reduce_fusion.26
  460.8 4.4 multiply_reduce_fusion.37
  465.2 4.4 multiply_reduce_fusion.48
  469.6 37.4 %select_convert_fusion = bf16[4,256,256]{2,1,0:T(8,128)(2,1)} fusion(f32[4,256,256]{2,1,0:T(8,128)} %get-tuple-element.291, f32[4,256,256]{2,1,0:T(8,128)} %get-tuple-element.292, f32[4,256,256]{2,1,0:T(8,128)} %get-tuple-element.293, f32[4,256,256]{2,1,0:T(8,128)} %get-tuple-element.294, f32[4,256,256]{2,1,0:T(8,128)} %get-tuple-element.295, ...), kind=kLoop, calls=%fused_computation.704 | loop fusion | flops 34865152 | bytes 6882336 | tf_op jit(solution)/shard_map/convert_element_type | solution.py:250
  513.2 6.1 multiply_reduce_fusion.70
  519.3 4.5 multiply_reduce_fusion.81
  523.8 4.4 multiply_reduce_fusion.92
  528.2 4.4 multiply_reduce_fusion.103
  532.7 4.4 multiply_reduce_fusion.114
  542.3 4.4 fusion.1
  546.8 41.9 %select_convert_fusion.1 = bf16[4,256,256]{2,1,0:T(8,128)(2,1)} fusion(f32[4,256,256]{2,1,0:T(8,128)} %get-tuple-element.296, f32[4,256,256]{2,1,0:T(8,128)} %get-tuple-element.297, f32[4,256,256]{2,1,0:T(8,128)} %get-tuple-element.298, f32[4,256,256]{2,1,0:T(8,128)} %get-tuple-element.299, f32[4,256,256]{2,1,0:T(8,128)} %get-tuple-element.300, ...), kind=kLoop, calls=%fused_computation.707 | loop fusion | flops 34865152 | bytes 6882336 | tf_op jit(solution)/shard_map/convert_element_type | solution.py:250
  600.2 4.4 fusion
  604.7 4.0 convolution_convert_fusion.2
  611.4 4.0 add_bitcast_fusion
  615.4 10.8 %copy.431 = f32[3,1536,384]{2,0,1:T(4,128)} copy(f32[3,1536,384]{1,2,0:T(8,128)} %add_bitcast_fusion) | data formatting | bytes 14155776
  626.2 7.2 copy.434
  640.4 3.7 convolution_add_fusion
  646.6 3.6 convolution_add_fusion.1
  652.8 3.6 convolution_add_fusion.2
  703.3 5.1 multiply_reduce_fusion.125
  785.8 11.7 %convolution_bitcast_fusion.4 = f32[2,2,2]{2,1,0:T(2,128)S(1)} fusion(f32[2,2,256,256]{3,2,1,0:T(8,128)S(1)} %bitcast.407, f32[2,2,256,256]{3,2,1,0:T(8,128)S(1)} %bitcast.409), kind=kOutput, calls=%fused_computation.301 | convolution fusion | flops 6291456 | bytes 2097184 | tf_op jit(solution)/shard_map/gaij,gbij->gab/dot_general | solution.py:239
  797.7 10.9 %fusion.12 = f32[2,2,2]{2,1,0:T(2,128)S(1)} fusion(f32[2,2,2]{2,1,0:T(2,128)S(1)} %convolution_bitcast_fusion.4, f32[2,2,256,256]{3,2,1,0:T(8,128)S(1)} %bitcast.405, f32[2,2,256,256]{3,2,1,0:T(8,128)S(1)} %bitcast.411), kind=kOutput, calls=%fused_computation.303 | convolution fusion | flops 6291464 | bytes 2097216 | tf_op jit(solution)/shard_map/gaij,gbij->gab/dot_general | solution.py:239
  810.3 23.4 %all-reduce.20 = (f32[1536]{0:T(1024)S(1)}, f32[4,6,11]{2,0,1:T(4,128)}, f32[2,2,2]{2,1,0:T(2,128)}, f32[384]{0:T(512)}, f32[1536]{0:T(1024)S(1)}) all-reduce(f32[1536]{0:T(1024)S(1)} %add.1424, f32[4,6,11]{2,0,1:T(4,128)S(1)} %add.1416, f32[2,2,2]{2,1,0:T(2,128)S(1)} %fusion.12, ...), channel_id=19, replica_groups=mesh['dp'=8,'mp'=4] {'dp'}, use_global_device_ids=true, to_apply=%region_39.40.clone | all-reduce | flops 3728 | bytes 29824
  833.8 11.2 %all-reduce.21 = (f32[192]{0:T(256)}, f32[192]{0:T(256)}) all-reduce(f32[192]{0:T(256)S(1)} %dynamic-slice.3, f32[192]{0:T(256)S(1)} %dynamic-slice.5), channel_id=1, replica_groups=mesh['dp'=8,'mp'=4] {'mp'}, use_global_device_ids=true, to_apply=%region_42.43 | all-reduce | flops 384 | bytes 3072 | tf_op jit(solution)/shard_map/psum | solution.py:298
  851.3 48.2 %reduce-scatter.36.cloned.1.call-done = f32[192,1024]{1,0:T(8,128)} async-done(((f32[1536,1024]{1,0:T(8,128)}), f32[192,1024]{1,0:T(8,128)}) %reduce-scatter.36.cloned.1.call-update) | async-done | bytes 786448 | tf_op jit(solution)/shard_map/reduce_scatter | solution.py:294
  899.5 65.6 %reduce-scatter.34.cloned.1.call-done = f32[192,1024]{1,0:T(8,128)} async-done(((f32[1536,1024]{1,0:T(8,128)}), f32[192,1024]{1,0:T(8,128)}) %reduce-scatter.34.cloned.1.call-update) | async-done | bytes 786448 | tf_op jit(solution)/shard_map/reduce_scatter | solution.py:293
  (625 shorter events, 259.0 us)
Async XLA Ops:
  7.2 35.3 %copy-start.1 = (bf16[2,1,64,1536]{3,2,1,0:T(8,128)(2,1)S(1)}, bf16[2,1,64,1536]{3,2,1,0:T(8,128)(2,1)}, u32[]{:S(2)}) copy-start(bf16[2,1,64,1536]{3,2,1,0:T(8,128)(2,1)} %param.13) | copy-start | bytes 1179652
  7.2 71.2 %all-gather.8.cloned.1.call-start = ((), (), s32[]{:S(2)}) async-start(), calls=%async_computation.13 | async-start | bytes 3981312 | tf_op jit(solution)/shard_map/all_gather | solution.py:134
  7.9 132.9 %all-gather.10.cloned.1.call-start = ((), (), s32[]{:S(2)}) async-start(), calls=%async_computation.14 | async-start | bytes 1327104 | tf_op jit(solution)/shard_map/all_gather | solution.py:135
  8.7 193.9 %reduce-scatter.16.cloned.1.call-start = ((), (), s32[]{:S(2)}) async-start(), calls=%async_computation.15 | async-start | bytes 983040 | tf_op jit(solution)/shard_map/reduce_scatter | solution.py:169
  12.7 76.8 %copy-start.81 = (f32[4]{0:T(128)}, f32[4]{0:T(128)S(1)}, u32[]{:S(2)}) copy-start(f32[4]{0:T(128)S(1)} %get-tuple-element.231) | copy-start | bytes 52
  20.4 69.1 %copy-start.68 = (pred[256,256]{1,0:T(8,128)(4,1)}, pred[256,256]{1,0:T(8,128)(4,1)S(1)}, u32[]{:S(2)}) copy-start(pred[256,256]{1,0:T(8,128)(4,1)S(1)} %fusion.334) | copy-start | bytes 196612
  21.8 60.1 %copy-start.139 = (f32[64]{0:T(128)}, f32[64]{0:T(128)S(1)}, u32[]{:S(2)}) copy-start(f32[64]{0:T(128)S(1)} %add_rsqrt_fusion.5) | copy-start | bytes 772
  21.8 60.1 %copy-start.137 = (f32[64]{0:T(128)}, f32[64]{0:T(128)S(1)}, u32[]{:S(2)}) copy-start(f32[64]{0:T(128)S(1)} %add_rsqrt_fusion.3) | copy-start | bytes 772
  22.5 125.3 %copy-start.74 = (f32[384]{0:T(512)}, f32[384]{0:T(512)S(1)}, u32[]{:S(2)}) copy-start(f32[384]{0:T(512)S(1)} %convert_element_type.297) | copy-start | bytes 4612
  109.7 26.2 %copy-start.3 = (f32[4,256,256]{2,1,0:T(8,128)}, f32[4,256,256]{2,1,0:T(8,128)S(1)}, u32[]{:S(2)}) copy-start(f32[4,256,256]{2,1,0:T(8,128)S(1)} %get-tuple-element.304) | copy-start | bytes 3145732
  110.1 25.8 %copy-start.77 = (f32[4,256]{1,0:T(4,128)}, f32[4,256]{1,0:T(4,128)S(1)}, u32[]{:S(2)}) copy-start(f32[4,256]{1,0:T(4,128)S(1)} %log_add_fusion.1) | copy-start | bytes 12292
  143.8 61.9 %reduce-scatter.20.cloned.1.call-start = ((), (), s32[]{:S(2)}) async-start(), calls=%async_computation.20 | async-start | bytes 983040 | tf_op jit(solution)/shard_map/reduce_scatter | solution.py:169
  150.8 94.4 %all-gather.14.cloned.1.call-start = ((), (), s32[]{:S(2)}) async-start(), calls=%async_computation.17 | async-start | bytes 3538944 | tf_op jit(solution)/shard_map/all_gather | solution.py:138
  151.4 124.1 %all-gather.12.cloned.1.call-start = ((), (), s32[]{:S(2)}) async-start(), calls=%async_computation.16 | async-start | bytes 3538944 | tf_op jit(solution)/shard_map/all_gather | solution.py:137
  151.9 157.8 %all-gather.16.cloned.1.call-start = ((), (), s32[]{:S(2)}) async-start(), calls=%async_computation.18 | async-start | bytes 3538944 | tf_op jit(solution)/shard_map/all_gather | solution.py:139
  152.7 189.8 %reduce-scatter.24.cloned.1.call-start = ((), (), s32[]{:S(2)}) async-start(), calls=%async_computation.22 | async-start | bytes 983040 | tf_op jit(solution)/shard_map/reduce_scatter | solution.py:201
  206.9 186.3 %copy-start.135 = (f32[64]{0:T(128)}, f32[64]{0:T(128)S(1)}, u32[]{:S(2)}) copy-start(f32[64]{0:T(128)S(1)} %add_rsqrt_fusion.4) | copy-start | bytes 772
  206.9 186.3 %copy-start.133 = (f32[64]{0:T(128)}, f32[64]{0:T(128)S(1)}, u32[]{:S(2)}) copy-start(f32[64]{0:T(128)S(1)} %add_rsqrt_fusion.2) | copy-start | bytes 772
  227.1 48.4 %copy-start.11 = (bf16[256,1536]{1,0:T(8,128)(2,1)}, bf16[256,1536]{1,0:T(8,128)(2,1)S(1)}, u32[]{:S(2)}) copy-start(bf16[256,1536]{1,0:T(8,128)(2,1)S(1)} %all_gather.57) | copy-start | bytes 2359300
  318.9 48.9 %reduce-scatter.28.cloned.1.call-start = ((), (), s32[]{:S(2)}) async-start(), calls=%async_computation.24 | async-start | bytes 983040 | tf_op jit(solution)/shard_map/reduce_scatter | solution.py:201
  330.7 62.5 %reduce-scatter.22.cloned.1.call-start = ((), (), s32[]{:S(2)}) async-start(), calls=%async_computation.21 | async-start | bytes 983040 | tf_op jit(solution)/shard_map/reduce_scatter | solution.py:184
  330.8 37.1 %copy-start.26 = (bf16[64,1536]{1,0:T(8,128)(2,1)S(1)}, bf16[64,1536]{1,0:T(8,128)(2,1)}, u32[]{:S(2)}) copy-start(bf16[64,1536]{1,0:T(8,128)(2,1)} %reduce-scatter.16.cloned.1.call-done) | copy-start | bytes 589828
  330.8 37.1 %copy-start.28 = (bf16[64,1536]{1,0:T(8,128)(2,1)S(1)}, bf16[64,1536]{1,0:T(8,128)(2,1)}, u32[]{:S(2)}) copy-start(bf16[64,1536]{1,0:T(8,128)(2,1)} %reduce-scatter.20.cloned.1.call-done) | copy-start | bytes 589828
  334.8 473.8 %reduce-scatter.30.cloned.1.call-start = ((), (), s32[]{:S(2)}) async-start(), calls=%async_computation.25 | async-start | bytes 983040 | tf_op jit(solution)/shard_map/reduce_scatter | solution.py:265
  369.8 43.8 %copy-start.146 = (f32[64]{0:T(128)}, f32[64]{0:T(128)S(1)}, u32[]{:S(2)}) copy-start(f32[64]{0:T(128)S(1)} %broadcast_multiply_fusion.21) | copy-start | bytes 772
  369.8 43.7 %copy-start.144 = (f32[64]{0:T(128)}, f32[64]{0:T(128)S(1)}, u32[]{:S(2)}) copy-start(f32[64]{0:T(128)S(1)} %broadcast_multiply_fusion.19) | copy-start | bytes 772
  369.8 43.7 %copy-start.23 = (f32[256,384]{1,0:T(8,128)S(1)}, f32[256,384]{1,0:T(8,128)}, u32[]{:S(2)}) copy-start(f32[256,384]{1,0:T(8,128)} %copy-done.22) | copy-start | bytes 1179652
  369.8 43.7 %copy-start.75 = (f32[384]{0:T(512)S(1)}, f32[384]{0:T(512)}, u32[]{:S(2)}) copy-start(f32[384]{0:T(512)} %copy-done.74) | copy-start | bytes 4612
  546.7 261.9 %reduce-scatter.26.cloned.1.call-start = ((), (), s32[]{:S(2)}) async-start(), calls=%async_computation.23 | async-start | bytes 983040 | tf_op jit(solution)/shard_map/reduce_scatter | solution.py:265
  604.6 240.4 %reduce-scatter.18.cloned.1.call-start = ((), (), s32[]{:S(2)}) async-start(), calls=%async_computation.19 | async-start | bytes 983040 | tf_op jit(solution)/shard_map/reduce_scatter | solution.py:184
  608.7 240.1 %reduce-scatter.40.cloned.1.call-start = ((), (), s32[]{:S(2)}) async-start(), calls=%async_computation.30 | async-start | bytes 7962624
  633.5 217.8 %reduce-scatter.32.cloned.1.call-start = ((), (), s32[]{:S(2)}) async-start(), calls=%async_computation.26 | async-start | bytes 2654208 | tf_op jit(solution)/shard_map/reduce_scatter | solution.py:291
  637.8 213.4 %reduce-scatter.38.cloned.1.call-start = ((), (), s32[]{:S(2)}) async-start(), calls=%async_computation.29 | async-start | bytes 7077888 | tf_op jit(solution)/shard_map/reduce_scatter | solution.py:295
  644.1 255.4 %reduce-scatter.36.cloned.1.call-start = ((), (), s32[]{:S(2)}) async-start(), calls=%async_computation.28 | async-start | bytes 7077888 | tf_op jit(solution)/shard_map/reduce_scatter | solution.py:294
  650.3 314.8 %reduce-scatter.34.cloned.1.call-start = ((), (), s32[]{:S(2)}) async-start(), calls=%async_computation.27 | async-start | bytes 7077888 | tf_op jit(solution)/shard_map/reduce_scatter | solution.py:293
  689.2 96.6 %copy-start.38 = (f32[4,256,256]{2,1,0:T(8,128)S(1)}, f32[4,256,256]{2,1,0:T(8,128)}, u32[]{:S(2)}) copy-start(f32[4,256,256]{2,1,0:T(8,128)} %copy-done.36) | copy-start | bytes 3145732
  689.2 96.6 %copy-start.40 = (f32[4,256,256]{2,1,0:T(8,128)S(1)}, f32[4,256,256]{2,1,0:T(8,128)}, u32[]{:S(2)}) copy-start(f32[4,256,256]{2,1,0:T(8,128)} %copy-done.39) | copy-start | bytes 3145732
  797.6 47.4 %copy-start.27 = (bf16[64,1536]{1,0:T(8,128)(2,1)S(1)}, bf16[64,1536]{1,0:T(8,128)(2,1)}, u32[]{:S(2)}) copy-start(bf16[64,1536]{1,0:T(8,128)(2,1)} %reduce-scatter.16.cloned.1.call-done) | copy-start | bytes 589828
  797.6 47.4 %copy-start.47 = (bf16[2,1,64,1536]{3,2,1,0:T(8,128)(2,1)S(1)}, bf16[2,1,64,1536]{3,2,1,0:T(8,128)(2,1)}, u32[]{:S(2)}) copy-start(bf16[2,1,64,1536]{3,2,1,0:T(8,128)(2,1)} %param.14) | copy-start | bytes 1179652
  797.6 47.4 %copy-start.65 = (bf16[64,1536]{1,0:T(8,128)(2,1)S(1)}, bf16[64,1536]{1,0:T(8,128)(2,1)}, u32[]{:S(2)}) copy-start(bf16[64,1536]{1,0:T(8,128)(2,1)} %reduce-scatter.24.cloned.1.call-done) | copy-start | bytes 589828
  797.6 47.4 %copy-start.136 = (f32[64]{0:T(128)S(1)}, f32[64]{0:T(128)}, u32[]{:S(2)}) copy-start(f32[64]{0:T(128)} %copy-done.135) | copy-start | bytes 772
  797.7 47.4 %copy-start.147 = (f32[64]{0:T(128)S(1)}, f32[64]{0:T(128)}, u32[]{:S(2)}) copy-start(f32[64]{0:T(128)} %copy-done.146) | copy-start | bytes 772
  808.5 38.1 %copy-start.73 = (bf16[1,64,1536]{2,1,0:T(8,128)(2,1)S(1)}, bf16[1,64,1536]{2,1,0:T(8,128)(2,1)}, u32[]{:S(2)}) copy-start(bf16[1,64,1536]{2,1,0:T(8,128)(2,1)} %get-tuple-element.313) | copy-start | bytes 589828
  808.5 38.8 %copy-start.29 = (bf16[64,1536]{1,0:T(8,128)(2,1)S(1)}, bf16[64,1536]{1,0:T(8,128)(2,1)}, u32[]{:S(2)}) copy-start(bf16[64,1536]{1,0:T(8,128)(2,1)} %reduce-scatter.20.cloned.1.call-done) | copy-start | bytes 589828
  808.6 38.8 %copy-start.66 = (bf16[64,1536]{1,0:T(8,128)(2,1)S(1)}, bf16[64,1536]{1,0:T(8,128)(2,1)}, u32[]{:S(2)}) copy-start(bf16[64,1536]{1,0:T(8,128)(2,1)} %reduce-scatter.28.cloned.1.call-done) | copy-start | bytes 589828
  808.6 38.8 %copy-start.134 = (f32[64]{0:T(128)S(1)}, f32[64]{0:T(128)}, u32[]{:S(2)}) copy-start(f32[64]{0:T(128)} %copy-done.133) | copy-start | bytes 772
  808.6 38.8 %copy-start.145 = (f32[64]{0:T(128)S(1)}, f32[64]{0:T(128)}, u32[]{:S(2)}) copy-start(f32[64]{0:T(128)} %copy-done.144) | copy-start | bytes 772
  808.6 38.8 %copy-start.72 = (bf16[64,1536]{1,0:T(8,128)(2,1)S(1)}, bf16[64,1536]{1,0:T(8,128)(2,1)}, u32[]{:S(2)}) copy-start(bf16[64,1536]{1,0:T(8,128)(2,1)} %reduce-scatter.30.cloned.1.call-done) | copy-start | bytes 589828
  (119 other events, 433.2 us)
Sparse Core Ops, SparseCore 0:
  9.9 36.9 all-gather.7
  48.8 24.0 all-gather.9
  143.9 30.7 reduce-scatter.15
  177.4 28.1 reduce-scatter.19
  207.3 34.0 all-gather.13
  243.2 32.3 all-gather.11
  277.4 32.3 all-gather.15
  319.1 23.3 reduce-scatter.23
  345.3 22.4 reduce-scatter.27
  370.6 22.5 reduce-scatter.21
  546.9 23.1 reduce-scatter.29
  604.7 23.1 reduce-scatter.25
  630.2 22.5 reduce-scatter.17
  656.2 64.8 reduce-scatter.39
  725.2 42.4 reduce-scatter.31
  771.5 61.9 reduce-scatter.37
  837.6 61.8 reduce-scatter.35
  903.3 61.7 reduce-scatter.33
where the time goes:
time: 980 us; the launch traced here: 972 us
  waiting for transfers between devices  233 us (24%)
  blocking collectives  209 us (21%)
  other arithmetic  206 us (21%)
  local copies, waits for them, and re-layouts  179 us (18%)
  matrix products  125 us (13%)
  between operations  18 us (2%)
    another operation x144, local copies, waits for them, and re-layouts, conv_backward(): kernel_rows.append(jnp.stack(taps, axis=1))  118 us
    convert_element_type x2, other arithmetic, shards(): grad_scores = jnp.where(mask[None], grad_zeroed, 0.0).astype(jnp.bfloat16)  79.4 us
    reduce_scatter x1, waiting for transfers between devices, shards(): lax.psum_scatter(local_grads[4], 'dp', scatter_dimension=0, tiled=True)  65.6 us
    all_gather x2, blocking collectives, shards(): all_grad = lax.all_gather(grad_rows, 'mp', axis=0, tiled=True)  49.8 us
    reduce_scatter x1, waiting for transfers between devices, shards(): lax.psum_scatter(local_grads[5], 'dp', scatter_dimension=0, tiled=True)  48.2 us
    reduce_sum x10, other arithmetic, conv_backward(): jnp.sum(weighted * earlier_rows[:, :, CK - 1 - key_shift:CK - 1 - key_shi...  44.1 us
    reduce_max x2, other arithmetic, shards(): top = jnp.max(masked, axis=-1, keepdims=True)  41.8 us
    unnamed x2, blocking collectives  39.6 us
  transfers between devices with their start and end apart: 18, of which 8 were waited for; matrix products, arithmetic and copies ran while one was open for 39% of the time, Pallas kernels for 0%

commit v1 on v0

v1 whole, which is shorter than its diff:
```python
import functools
import math

import jax
import jax.numpy as jnp
from jax import lax
from jax.experimental import pallas as pl
from jax.experimental.pallas import tpu as pltpu
from jax.sharding import PartitionSpec as P

CQ = 6
CK = 11
CENTER = CK // 2
EPS = 1e-05
F32 = jnp.float32
BF16 = jnp.bfloat16
VMEM_LIMIT = 58 * 1024 * 1024

NN = (((1,), (0,)), ((), ()))
NT = (((1,), (1,)), ((), ()))
TN = (((0,), (0,)), ((), ()))


def mm(left, right, dims=NN):
    return lax.dot_general(left, right, dims, preferred_element_type=F32)


def spec_vmem():
    return pl.BlockSpec(memory_space=pltpu.VMEM)


def spec_smem():
    return pl.BlockSpec(memory_space=pltpu.SMEM)


def call(body, outs, ins, scratch=(), smem=0, flops=0, name=None):
    nbytes = sum(math.prod(a.shape) * a.dtype.itemsize for a in list(ins) + list(outs))
    return pl.pallas_call(
        body,
        out_shape=outs,
        in_specs=[spec_smem()] * smem + [spec_vmem()] * (len(ins) - smem),
        out_specs=[spec_vmem()] * len(outs),
        scratch_shapes=list(scratch),
        compiler_params=pltpu.CompilerParams(vmem_limit_bytes=VMEM_LIMIT),
        cost_estimate=pl.CostEstimate(flops=flops, bytes_accessed=nbytes, transcendentals=0),
        name=name,
    )(*ins)


def sds(shape, dtype):
    return jax.ShapeDtypeStruct(shape, dtype)


def segment_ids(lengths, length):
    ends = jnp.cumsum(lengths)
    places = jnp.arange(length, dtype=jnp.int32)
    return jnp.sum((places[:, None] >= ends[None, :]).astype(jnp.int32), axis=1)


def place(me, step, parts, rows):
    return pl.multiple_of(lax.rem(me - step + parts, parts) * rows, rows)


def masks(seg_col, seg_row, length):
    same = seg_col == seg_row
    row = lax.broadcasted_iota(jnp.int32, (length, length), 0)
    col = lax.broadcasted_iota(jnp.int32, (length, length), 1)
    return same, same & (col <= row)


def shift_rows(values, shift, same):
    if shift == 0:
        return values.astype(BF16)
    length = values.shape[0]
    return jnp.where(same, pltpu.roll(values, shift % length, 0), 0.0).astype(BF16)


def head_norm(heads_out):
    centered = heads_out - jnp.mean(heads_out, axis=-1, keepdims=True)
    inv_std = lax.rsqrt(jnp.mean(centered * centered, axis=-1, keepdims=True) + EPS)
    return centered * inv_std, inv_std


def attn_fwd_body(cfg, me_ref, mix_ref, *refs):
    parts, rows, heads, size = cfg
    x_refs = refs[:parts]
    w_ref, band_ref, segc_ref, segr_ref, ggain_ref = refs[parts : parts + 5]
    outs = refs[parts + 5 :]
    att_refs = outs[:parts]
    normed_ref, qkv_ref, z_ref, p_ref, ho_ref, grouped_ref, gains_ref, att_scr = outs[parts:]
    length = parts * rows
    width = heads * size
    me = me_ref[0]
    gains = w_ref[:, 4 * width :].astype(F32).T
    gains_ref[...] = gains[:8]
    gain = gains[0:1]
    for step in range(parts):
        x = x_refs[step][...].astype(F32)
        r1 = lax.rsqrt(jnp.mean(x * x, axis=-1, keepdims=True) + EPS)
        normed_ref[pl.ds(place(me, step, parts, rows), rows), :] = (x * r1 * gain).astype(BF16)
    qkv_ref[...] = mm(normed_ref[...], w_ref[:, : 3 * width]).astype(BF16)
    same, allow = masks(segc_ref[...], segr_ref[...], length)
    scale = 1.0 / math.sqrt(size)
    for pair in range(heads // 2):
        probs = []
        for b in range(2):
            h = 2 * pair + b
            q = qkv_ref[:, h * size : (h + 1) * size]
            k = qkv_ref[:, width + h * size : width + (h + 1) * size]
            z = jnp.where(allow, mm(q, k, NT) * scale, 0.0)
            z_ref[h] = z.astype(BF16)
            acc = jnp.zeros((length, length), F32)
            for a in range(CQ):
                acc = acc + mm(shift_rows(z, a, same), band_ref[h * CQ + a])
            logits = jnp.where(allow, acc, -jnp.inf)
            e = jnp.exp(logits - jnp.max(logits, axis=-1, keepdims=True))
            p = e * (1.0 / jnp.sum(e, axis=-1, keepdims=True))
            p_ref[h] = p
            probs.append(p)
        for a in range(2):
            h = 2 * pair + a
            mixed = (
                mix_ref[4 * pair + 2 * a] * probs[0] + mix_ref[4 * pair + 2 * a + 1] * probs[1]
            ).astype(BF16)
            v = qkv_ref[:, 2 * width + h * size : 2 * width + (h + 1) * size]
            ho = mm(mixed, v)
            ho_ref[h] = ho
            normed, _ = head_norm(ho)
            grouped_ref[:, h * size : (h + 1) * size] = (
                normed * ggain_ref[:, h * size : (h + 1) * size]
            ).astype(BF16)
    att_scr[...] = mm(grouped_ref[...], w_ref[:, 3 * width : 4 * width], NT)
    for step in range(parts):
        att_refs[step][...] = att_scr[pl.ds(place(me, step, parts, rows), rows), :].astype(BF16)


def attn_fwd(me, mix, xs, w1, band, segc, segr, ggain, heads, size):
    parts = len(xs)
    rows, d = xs[0].shape
    length, width = parts * rows, heads * size
    outs = (
        [sds((rows, d), BF16)] * parts
        + [
            sds((length, d), BF16),
            sds((length, 3 * width), BF16),
            sds((heads, length, length), BF16),
            sds((heads, length, length), F32),
            sds((heads, length, size), F32),
            sds((length, width), BF16),
            sds((8, d), F32),
        ]
    )
    res = call(
        functools.partial(attn_fwd_body, (parts, rows, heads, size)),
        outs,
        [me, mix, *xs, w1, band, segc, segr, ggain],
        scratch=[pltpu.VMEM((length, d), F32)],
        smem=2,
        flops=2 * length * d * width * 4 + 2 * heads * (CQ + 2) * length**3,
        name="attn_fwd",
    )
    return res[:parts], res[parts:]


def tail_rms(values, gain):
    r = lax.rsqrt(jnp.mean(values * values, axis=-1, keepdims=True) + EPS)
    return values * r, r


def rms_back(grad, normal, r, gain):
    u = grad * gain
    return r * (u - normal * jnp.mean(u * normal, axis=-1, keepdims=True))


def total(refs):
    acc = refs[0][...].astype(F32)
    for ref in refs[1:]:
        acc = acc + ref[...].astype(F32)
    return acc


def mid_body(parts, *refs):
    x_ref, gains_ref = refs[:2]
    hid_ref, mid_ref = refs[2 + parts :]
    hidden_in = x_ref[...].astype(F32) + total(refs[2 : 2 + parts])
    hid_ref[...] = hidden_in
    normal, _ = tail_rms(hidden_in, None)
    mid_ref[...] = (normal * gains_ref[1:2]).astype(BF16)


def mid_step(x, gains, pieces):
    return call(
        functools.partial(mid_body, len(pieces)),
        [sds(x.shape, F32), sds(x.shape, BF16)],
        [x, gains, *pieces],
        name="mid_step",
    )


def mid_back_body(parts, *refs):
    hid_ref, dy_ref, gains_ref = refs[:3]
    ghid_ref, ga_ref, gain_ref = refs[3 + parts :]
    gain = gains_ref[1:2]
    normal, r = tail_rms(hid_ref[...], None)
    grad = total(refs[3 : 3 + parts])
    gain_ref[...] = jnp.sum(grad * normal, axis=0, keepdims=True)
    ghid = dy_ref[...].astype(F32) + rms_back(grad, normal, r, gain)
    ghid_ref[...] = ghid
    ga_ref[...] = ghid.astype(BF16)


def mid_back(hid, dy, gains, pieces):
    return call(
        functools.partial(mid_back_body, len(pieces)),
        [sds(hid.shape, F32), sds(hid.shape, BF16), sds((1, hid.shape[1]), F32)],
        [hid, dy, gains, *pieces],
        name="mid_back",
    )


def last_body(parts, *refs):
    x_ref, ghid_ref, gains_ref = refs[:3]
    out_ref = refs[3 + parts]
    normal, r = tail_rms(x_ref[...].astype(F32), None)
    grad = total(refs[3 : 3 + parts])
    out_ref[...] = ghid_ref[...] + rms_back(grad, normal, r, gains_ref[0:1])


def last_step(x, ghid, gains, pieces):
    return call(
        functools.partial(last_body, len(pieces)),
        [sds(x.shape, F32)],
        [x, ghid, gains, *pieces],
        name="last_step",
    )[0]


def ffn_body(parts, rows, *refs):
    m_refs, dy_refs = refs[:parts], refs[parts : 2 * parts]
    wg_ref, wu_ref, wd_ref = refs[2 * parts : 2 * parts + 3]
    rest = refs[2 * parts + 3 :]
    o_refs, g_refs = rest[:parts], rest[parts : 2 * parts]
    mid_ref, dya_ref, hid_ref, gg_ref, gu_ref, out_acc, gmid_acc = rest[2 * parts :]
    j = pl.program_id(0)

    @pl.when(j == 0)
    def _():
        for step in range(parts):
            mid_ref[step * rows : (step + 1) * rows, :] = m_refs[step][...]
            dya_ref[step * rows : (step + 1) * rows, :] = dy_refs[step][...]
        out_acc[...] = jnp.zeros_like(out_acc)
        gmid_acc[...] = jnp.zeros_like(gmid_acc)

    mid = mid_ref[...]
    gate = mm(mid, wg_ref[...])
    up = mm(mid, wu_ref[...])
    gh = mm(dya_ref[...], wd_ref[...])
    sig = jax.nn.sigmoid(gate)
    swish = gate * sig
    hidden = (swish * up).astype(BF16)
    hid_ref[...] = hidden
    gg = (gh * up * sig * (1.0 + gate * (1.0 - sig))).astype(BF16)
    gu = (gh * swish).astype(BF16)
    gg_ref[...] = gg
    gu_ref[...] = gu
    gmid_acc[...] += mm(gg, wg_ref[...], NT) + mm(gu, wu_ref[...], NT)
    out_acc[...] += mm(hidden, wd_ref[...], NT)

    @pl.when(j == pl.num_programs(0) - 1)
    def _():
        for step in range(parts):
            o_refs[step][...] = out_acc[step * rows : (step + 1) * rows, :].astype(BF16)
            g_refs[step][...] = gmid_acc[step * rows : (step + 1) * rows, :].astype(BF16)


def ffn(ms, dys, w2):
    parts = len(ms)
    rows, d = ms[0].shape
    length = parts * rows
    ff = w2.shape[1] // 3
    cols = min(256, ff)
    steps = ff // cols
    whole = lambda shape: pl.BlockSpec(shape, lambda j: (0, 0))
    weight = lambda c: pl.BlockSpec((d, cols), lambda j, c=c: (0, c * steps + j))
    chunk = pl.BlockSpec((length, cols), lambda j: (0, j))
    outs = (
        [sds((rows, d), BF16)] * (2 * parts)
        + [sds((length, d), BF16)] * 2
        + [sds((length, ff), BF16)] * 3
    )
    res = pl.pallas_call(
        functools.partial(ffn_body, parts, rows),
        grid=(steps,),
        in_specs=[whole((rows, d))] * (2 * parts) + [weight(0), weight(1), weight(2)],
        out_specs=[whole((rows, d))] * (2 * parts) + [whole((length, d))] * 2 + [chunk] * 3,
        out_shape=outs,
        scratch_shapes=[pltpu.VMEM((length, d), F32)] * 2,
        compiler_params=pltpu.CompilerParams(vmem_limit_bytes=VMEM_LIMIT),
        cost_estimate=pl.CostEstimate(
            flops=2 * length * d * ff * 6, bytes_accessed=6 * d * ff, transcendentals=0
        ),
        name="ffn",
    )(*ms, *dys, w2, w2, w2)
    return res[:parts], res[parts : 2 * parts], res[2 * parts :]


def band_sum(values, length):
    lane = lax.broadcasted_iota(jnp.int32, (8, 128), 1)
    lane = jnp.where(lane >= 64, lane - 128, lane)
    acc = jnp.zeros((8, 128), F32)
    tiles = length // 128
    for s in range(length // 8):
        back = (128 - 8 * s % 128) % 128
        low, high = 8 * s - CENTER, 8 * s + 7 + CENTER
        first, last = max(low, 0) // 128, min(high, length - 1) // 128
        for tile in range(first, last + 1):
            piece = values[8 * s : 8 * s + 8, tile * 128 : (tile + 1) * 128]
            if back:
                piece = pltpu.roll(piece, back, 1)
            start, stop = tile * 128 - 8 * s, tile * 128 + 128 - 8 * s
            if low < tile * 128 or high >= tile * 128 + 128:
                piece = jnp.where((lane >= start) & (lane < stop), piece, 0.0)
            acc = acc + piece
    return acc


def attn_bwd_body(cfg, me_ref, mix_ref, *refs):
    parts, rows, heads, size = cfg
    ga_refs = refs[:parts]
    (w_ref, band_ref, segc_ref, segr_ref, ggain_ref, gains_ref, normed_ref, qkv_ref, z_ref,
     p_ref, ho_ref) = refs[parts : parts + 11]
    outs = refs[parts + 11 :]
    gi_refs = outs[:parts]
    (gaa_ref, gproj_ref, again_ref, ggrad_ref, kern_ref, mixg_ref, gin_scr, diag_scr) = outs[parts:]
    length = parts * rows
    width = heads * size
    me = me_ref[0]
    for step in range(parts):
        gaa_ref[pl.ds(place(me, step, parts, rows), rows), :] = ga_refs[step][...]
    gin_scr[:, :width] = mm(gaa_ref[...], w_ref[:, 3 * width : 4 * width])
    same, allow = masks(segc_ref[...], segr_ref[...], length)
    scale = 1.0 / math.sqrt(size)
    for pair in range(heads // 2):
        gmix = []
        for a in range(2):
            h = 2 * pair + a
            lanes = slice(h * size, (h + 1) * size)
            gg = gin_scr[:, lanes]
            normed, inv_std = head_norm(ho_ref[h])
            ggrad_ref[:, lanes] = jnp.sum(gg * normed, axis=0, keepdims=True)
            u = gg * ggain_ref[:, lanes]
            gh = inv_std * (
                u
                - jnp.mean(u, axis=-1, keepdims=True)
                - normed * jnp.mean(u * normed, axis=-1, keepdims=True)
            )
            gh = gh.astype(BF16)
            v = qkv_ref[:, 2 * width + h * size : 2 * width + (h + 1) * size]
            gmix.append(mm(gh, v, NT))
            mixed = (
                mix_ref[4 * pair + 2 * a] * p_ref[2 * pair]
                + mix_ref[4 * pair + 2 * a + 1] * p_ref[2 * pair + 1]
            ).astype(BF16)
            gproj_ref[:, 2 * width + h * size : 2 * width + (h + 1) * size] = mm(
                mixed, gh, TN
            ).astype(BF16)
        for b in range(2):
            h = 2 * pair + b
            p = p_ref[h]
            for a in range(2):
                mixg_ref[4 * pair + 2 * a + b : 4 * pair + 2 * a + b + 1, :] = jnp.sum(
                    gmix[a] * p, axis=0, keepdims=True
                )
            gp = mix_ref[4 * pair + b] * gmix[0] + mix_ref[4 * pair + 2 + b] * gmix[1]
            gl = p * (gp - jnp.sum(gp * p, axis=-1, keepdims=True))
            glt = gl.T.astype(BF16)
            z = z_ref[h].astype(F32)
            gz = jnp.zeros((length, length), F32)
            for a in range(CQ):
                gz = gz + mm(shift_rows(gl, -a, same), band_ref[h * CQ + a], NT)
                diag_scr[h * CQ + a] = band_sum(mm(glt, shift_rows(z, a, same)), length)
            gs = jnp.where(allow, gz, 0.0).astype(BF16)
            q = qkv_ref[:, h * size : (h + 1) * size]
            k = qkv_ref[:, width + h * size : width + (h + 1) * size]
            gproj_ref[:, h * size : (h + 1) * size] = (mm(gs, k) * scale).astype(BF16)
            gproj_ref[:, width + h * size : width + (h + 1) * size] = (
                mm(gs, q, TN) * scale
            ).astype(BF16)
    taps = diag_scr[:, 0, :]
    for r in range(1, 8):
        taps = taps + pltpu.roll(diag_scr[:, r, :], 128 - r, 1)
    kern_ref[...] = taps
    gin_scr[...] = mm(gproj_ref[...], w_ref[:, : 3 * width], NT)
    again_ref[...] = (
        jnp.sum(gin_scr[...] * normed_ref[...].astype(F32), axis=0, keepdims=True) / gains_ref[0:1]
    )
    for step in range(parts):
        gi_refs[step][...] = gin_scr[pl.ds(place(me, step, parts, rows), rows), :].astype(BF16)


def attn_bwd(me, mix, gas, w1, band, segc, segr, ggain, gains, saved, heads, size):
    parts = len(gas)
    rows, d = gas[0].shape
    length, width = parts * rows, heads * size
    outs = (
        [sds((rows, d), BF16)] * parts
        + [
            sds((length, d), BF16),
            sds((length, 3 * width), BF16),
            sds((1, d), F32),
            sds((1, width), F32),
            sds((heads * CQ, 128), F32),
            sds((2 * heads, length), F32),
        ]
    )
    res = call(
        functools.partial(attn_bwd_body, (parts, rows, heads, size)),
        outs,
        [me, mix, *gas, w1, band, segc, segr, ggain, gains, *saved],
        scratch=[pltpu.VMEM((length, d), F32), pltpu.VMEM((heads * CQ, 8, 128), F32)],
        smem=2,
        flops=2 * length * d * width * 4 + 2 * heads * (2 * CQ + 4) * length**3,
        name="attn_bwd",
    )
    return res[:parts], res[parts:]


def gather_mp(part, size):
    return [part] + [
        lax.ppermute(part, "mp", [(i, (i + step) % size) for i in range(size)])
        for step in range(1, size)
    ]


def scatter_mp(pieces, size):
    return [pieces[0]] + [
        lax.ppermute(pieces[step], "mp", [(i, (i - step) % size) for i in range(size)])
        for step in range(1, size)
    ]


def sum_all(values, axis, size):
    bit = 1
    while bit < size:
        values = values + lax.ppermute(values, axis, [(i, i ^ bit) for i in range(size)])
        bit *= 2
    return values


def shards(
    block_input,
    out_grad,
    doc_lengths,
    attn_gain,
    qkv_weight,
    conv_kernel,
    head_mixing,
    group_gain,
    out_weight,
    mlp_gain,
    gate_weight,
    up_weight,
    down_weight,
):
    batches = block_input.shape[0]
    rows = block_input.shape[2]
    mp, dp = lax.axis_size("mp"), lax.axis_size("dp")
    length = rows * mp
    heads = conv_kernel.shape[0]
    width = qkv_weight.shape[2]
    size = width // heads
    local_d = attn_gain.shape[0]
    me = lax.axis_index("mp").astype(jnp.int32).reshape(1)
    mix = head_mixing.reshape(-1)
    ggain = group_gain.astype(F32)[None]

    gains_cols = jnp.pad(jnp.stack([attn_gain, mlp_gain], axis=1), ((0, 0), (0, 126)))
    pack1 = jnp.concatenate(
        [qkv_weight[0], qkv_weight[1], qkv_weight[2], out_weight.T, gains_cols], axis=1
    )
    pack2 = jnp.concatenate([gate_weight, up_weight, down_weight.T], axis=1)
    w1 = lax.all_gather(pack1, "dp", axis=0, tiled=True)
    w2 = lax.all_gather(pack2, "dp", axis=0, tiled=True)

    offset = (
        jnp.arange(length, dtype=jnp.int32)[None, :]
        - jnp.arange(length, dtype=jnp.int32)[:, None]
        + CENTER
    )
    band = jnp.zeros((heads * CQ, length, length), F32)
    taps = conv_kernel.reshape(heads * CQ, CK)
    for b in range(CK):
        band = jnp.where(offset[None] == b, taps[:, b][:, None, None], band)
    band = band.astype(BF16)

    outputs, input_grads, kept = [], [], []
    head_total = None
    for batch in range(batches):
        segment = segment_ids(doc_lengths[batch, 0], length)
        segc, segr = segment[:, None], segment[None, :]
        x, dy = block_input[batch, 0], out_grad[batch, 0]
        xs = gather_mp(x, mp)
        dys = gather_mp(dy, mp)
        pieces, saved = attn_fwd(me, mix, xs, w1, band, segc, segr, ggain, heads, size)
        normed, qkv, z, probs, ho, grouped, gains = saved
        hid, mid = mid_step(x, gains, scatter_mp(pieces, mp))
        mids = gather_mp(mid, mp)
        o_pieces, g_pieces, (mid_all, dy_all, hidden, gg, gu) = ffn(mids, dys, w2)
        ghid, ga, mlp_part = mid_back(hid, dy, gains, scatter_mp(g_pieces, mp))
        out = hid
        for piece in scatter_mp(o_pieces, mp):
            out = out + piece.astype(F32)
        outputs.append(out.astype(BF16))
        gas = gather_mp(ga, mp)
        gi_pieces, (ga_all, gproj, again, ggrad, kern, mixg) = attn_bwd(
            me, mix, gas, w1, band, segc, segr, ggain, gains, [normed, qkv, z, probs, ho], heads, size
        )
        input_grads.append(last_step(x, ghid, gains, scatter_mp(gi_pieces, mp)))
        small = (again, mlp_part, ggrad, kern, jnp.sum(mixg, axis=1))
        head_total = small if head_total is None else jax.tree.map(jnp.add, head_total, small)
        kept.append((mid_all, dy_all, hidden, gg, gu, normed, gproj, grouped, ga_all))

    mid_all, dy_all, hidden, gg, gu, normed, gproj, grouped, ga_all = (
        jnp.concatenate(group, axis=0) for group in zip(*kept)
    )
    grads2 = jnp.concatenate(
        [mm(mid_all, gg, TN), mm(mid_all, gu, TN), mm(dy_all, hidden, TN)], axis=1
    ).astype(BF16)
    share2 = lax.psum_scatter(grads2, "dp", scatter_dimension=0, tiled=True).astype(F32)
    grads1 = jnp.concatenate([mm(normed, gproj, TN), mm(ga_all, grouped, TN)], axis=1).astype(BF16)
    share1 = lax.psum_scatter(grads1, "dp", scatter_dimension=0, tiled=True).astype(F32)

    again, mlp_part, ggrad, kern, mixg = head_total
    d = again.shape[1]
    flat = jnp.concatenate([again[0], mlp_part[0], ggrad[0], kern.reshape(-1), mixg])
    count = flat.shape[0]
    flat = jnp.pad(flat, (0, -count % 128)).reshape(-1, 128)
    flat = sum_all(flat, "dp", dp).reshape(-1)
    gain_grads = sum_all(flat[: 2 * d].reshape(-1, 128), "mp", mp).reshape(2, dp, local_d)
    gain_grads = lax.dynamic_index_in_dim(gain_grads, lax.axis_index("dp"), 1, keepdims=False)
    ggrad = flat[2 * d : 2 * d + width]
    kern = flat[2 * d + width : 2 * d + width + heads * CQ * 128].reshape(heads, CQ, 128)
    kernel_grad = jnp.roll(kern, CK - 1 - CENTER, axis=2)[:, :, :CK][:, :, ::-1]
    mixing_grad = flat[2 * d + width + heads * CQ * 128 : count].reshape(heads // 2, 2, 2)
    ff = gate_weight.shape[1]
    return (
        jnp.stack(outputs)[:, None],
        jnp.stack(input_grads)[:, None],
        gain_grads[0],
        jnp.stack([share1[:, c * width : (c + 1) * width] for c in range(3)]),
        kernel_grad,
        mixing_grad,
        ggrad,
        share1[:, 3 * width :].T,
        gain_grads[1],
        share2[:, :ff],
        share2[:, ff : 2 * ff],
        share2[:, 2 * ff :].T,
    )


def solution(mesh):
    return jax.shard_map(
        shards,
        mesh=mesh,
        in_specs=(
            P(None, "dp", "mp", None),
            P(None, "dp", "mp", None),
            P(None, "dp", None),
            P("dp"),
            P(None, "dp", "mp"),
            P("mp", None, None),
            P("mp", None, None),
            P("mp"),
            P("mp", "dp"),
            P("dp"),
            P("dp", "mp"),
            P("dp", "mp"),
            P("mp", "dp"),
        ),
        out_specs=(
            P(None, "dp", "mp", None),
            P(None, "dp", "mp", None),
            P("dp"),
            P(None, "dp", "mp"),
            P("mp", None, None),
            P("mp", None, None),
            P("mp"),
            P("mp", "dp"),
            P("dp"),
            P("dp", "mp"),
            P("dp", "mp"),
            P("mp", "dp"),
        ),
        check_vma=False,
    )
```

time: 980 us -> 434 us (0.44)
  blocking collectives: 209 us -> 0 us
  other arithmetic: 206 us -> 22.8 us
  local copies, waits for them, and re-layouts: 179 us -> 56.5 us
  matrix products: 125 us -> 9.67 us
  starting transfers between devices: 1.11 us -> 99.7 us
  waiting for transfers between devices: 233 us -> 135 us
  Pallas kernels: 0 us -> 87.4 us
    reduce_scatter x12 -> x0, waiting for transfers between devices: 173 us -> none  [the longest x1 65.6 us: shards(): lax.psum_scatter(local_grads[4], 'dp', scatter_dimension=0, tiled=True)]
    all_gather x8 -> x0, blocking collectives: 158 us -> none  [the longest x2 49.8 us: shards(): all_grad = lax.all_gather(grad_rows, 'mp', axis=0, tiled=True)]
    another operation x153 -> x4, local copies, waits for them, and re-layouts: 129 us -> 1.47 us  [the longest x3 1.46 us: shards(): jnp.stack([attn_gain, mlp_gain], axis=1)]
    dot_general x44 -> x5, matrix products: 125 us -> 9.67 us  [mm(): return lax.dot_general(left, right, dims, preferred_element_type=F32)]
    ppermute x0 -> x53, waiting for transfers between devices: none -> 114 us  [the longest x24 55 us: scatter_mp(): lax.ppermute(pieces[step], 'mp', [(i, (i - step) % size) for i in range(s...]
    ppermute x0 -> x53, starting transfers between devices: none -> 99.5 us  [the longest x24 47.8 us: scatter_mp(): lax.ppermute(pieces[step], 'mp', [(i, (i - step) % size) for i in range(s...]
    pallas_call x0 -> x12, Pallas kernels: none -> 87.4 us  [the longest x10 62.5 us: call(): pl.pallas_call(body, out_shape=outs, in_specs=[spec_smem()] * smem + [spe...]
    convert_element_type x12 -> x3, other arithmetic: 85.3 us -> 9.09 us  [the longest x1 7.06 us: shards(): band = band.astype(BF16)]
  transfers between devices with their start and end apart: 18 -> 57, of which waited for: 8 -> 16; matrix products, arithmetic and copies ran while one was open for 39% -> 11% of each run, Pallas kernels for 0% -> 17%
where the time goes in v1:
time: 434 us; the launch traced here: 426 us
  waiting for transfers between devices  135 us (31%)
  starting transfers between devices  99.7 us (23%)
  Pallas kernels  87.4 us (20%)
  local copies, waits for them, and re-layouts  56.5 us (13%)
  other arithmetic  22.8 us (5%)
  between operations  15.3 us (4%)
  matrix products  9.67 us (2%)
    pallas_call x10, Pallas kernels, call(): pl.pallas_call(body, out_shape=outs, in_specs=[spec_smem()] * smem + [spe...  62.5 us
    ppermute x24, waiting for transfers between devices, scatter_mp(): lax.ppermute(pieces[step], 'mp', [(i, (i - step) % size) for i in range(s...  55 us
    ppermute x24, starting transfers between devices, scatter_mp(): lax.ppermute(pieces[step], 'mp', [(i, (i - step) % size) for i in range(s...  47.8 us
    ppermute x24, starting transfers between devices, gather_mp(): lax.ppermute(part, 'mp', [(i, (i + step) % size) for i in range(size)])  46.7 us
    unnamed x213, local copies, waits for them, and re-layouts  44.8 us
    ppermute x24, waiting for transfers between devices, gather_mp(): lax.ppermute(part, 'mp', [(i, (i + step) % size) for i in range(size)])  43.9 us
    pallas_call x2, Pallas kernels, ffn(): pl.pallas_call(functools.partial(ffn_body, parts, rows), grid=(steps,), i...  24.9 us
    unnamed x6, waiting for transfers between devices  19.7 us
  transfers between devices with their start and end apart: 57, of which 16 were waited for; matrix products, arithmetic and copies ran while one was open for 11% of the time, Pallas kernels for 17%

profile of v1, /device:TPU:0, one launch (start us, length us, event | category | flops | bytes accessed | tf_op | source)
XLA Modules:
  0.0 426.1 jit_solution(13338928485254871983)
XLA Ops:
  13.5 2.4 pad_maximum_fusion.2
  16.0 5.1 %collective-permute-start.2 = (bf16[64,1536]{1,0:T(8,128)(2,1)S(1)}, bf16[64,1536]{1,0:T(8,128)(2,1)S(1)}, u32[]{:S(2)}, u32[]{:S(2)}) collective-permute-start(bf16[64,1536]{1,0:T(8,128)(2,1)S(1)} %get-tuple-element.247.refs_0_), channel_id=1, source_target_pairs={{0,3},{1,0},{2,1},{3,2},{4,7},{5,4},{6,5},{7,6},{8,11},{9,8},{10,9... | collective-permute-start | bytes 589832 | tf_op jit(solution)/shard_map/ppermute | solution.py:430
  21.6 2.5 collective-permute-start.16
  28.4 7.1 %select_convert_fusion.refs_5_ = bf16[24,256,256]{2,1,0:T(8,128)(2,1)} fusion(bf16[24]{0:T(256)(128)(2,1)S(1)} %get-tuple-element.229, bf16[24]{0:T(256)(128)(2,1)S(1)} %get-tuple-element.230, bf16[24]{0:T(256)(128)(2,1)S(1)} %get-tuple-element.231, bf16[24]{0:T(256)(128)(2,1)S(1)} %get-tuple-element.232, bf16[24]{0:T(256)(128)(2,1)S(1)} %get-tuple-element.233, ...), kind=kLoop, calls=%fused_computation.2 | loop fusion | flops 17301504 | bytes 3867152 | tf_op jit(solution)/shard_map/convert_element_type | solution.py:494
  37.2 14.7 %collective-permute-start = (bf16[64,1536]{1,0:T(8,128)(2,1)S(1)}, bf16[64,1536]{1,0:T(8,128)(2,1)S(1)}, u32[]{:S(2)}, u32[]{:S(2)}) collective-permute-start(bf16[64,1536]{1,0:T(8,128)(2,1)S(1)} %get-tuple-element.247.refs_0_), channel_id=1, source_target_pairs={{0,1},{1,2},{2,3},{3,0},{4,5},{5,6},{6,7},{7,4},{8,9},{9,10},{10,1... | collective-permute-start | bytes 589832 | tf_op jit(solution)/shard_map/ppermute | solution.py:430
  51.9 3.1 collective-permute-done.16.refs_2_
  56.9 9.4 %attn_fwd.3 = (bf16[64,1536]{1,0:T(8,128)(2,1)}, bf16[64,1536]{1,0:T(8,128)(2,1)}, bf16[64,1536]{1,0:T(8,128)(2,1)}, bf16[64,1536]{1,0:T(8,128)(2,1)}, bf16[256,...) custom-call(s32[1]{0:T(128)} %bitcast.1.me_ref, ...), custom_call_target="tpu_custom_call" | custom-call | flops 2281701376 | bytes 13422116 | tf_op jit(solution)/shard_map/attn_fwd/pallas_call | solution.py:38
  66.3 3.4 collective-permute-start.18
  71.0 9.4 %attn_fwd.2 = (bf16[64,1536]{1,0:T(8,128)(2,1)}, bf16[64,1536]{1,0:T(8,128)(2,1)}, bf16[64,1536]{1,0:T(8,128)(2,1)}, bf16[64,1536]{1,0:T(8,128)(2,1)}, bf16[256,...) custom-call(s32[1]{0:T(128)} %bitcast.1.me_ref, ...), custom_call_target="tpu_custom_call" | custom-call | flops 2281701376 | bytes 13422116 | tf_op jit(solution)/shard_map/attn_fwd/pallas_call | solution.py:38
  80.4 2.9 collective-permute-start.3
  83.3 4.9 %collective-permute-done.19.refs_4_ = bf16[64,1536]{1,0:T(8,128)(2,1)S(1)} collective-permute-done((bf16[64,1536]{1,0:T(8,128)(2,1)}, bf16[64,1536]{1,0:T(8,128)(2,1)S(1)}, u32[]{:S(2)}, u32[]{:S(2)}) %collective-permute-start.19) | collective-permute-done | bytes 196640 | tf_op jit(solution)/shard_map/ppermute | solution.py:437
  88.2 9.0 %collective-permute-start.5 = (bf16[64,1536]{1,0:T(8,128)(2,1)}, bf16[64,1536]{1,0:T(8,128)(2,1)S(1)}, u32[]{:S(2)}, u32[]{:S(2)}) collective-permute-start(bf16[64,1536]{1,0:T(8,128)(2,1)} %get-tuple-element.94), channel_id=1, source_target_pairs={{0,1},{1,2},{2,3},{3,0},{4,5},{5,6},{6,7},{7,4},{8,9},{9,10},{10,1... | collective-permute-start | bytes 589832 | tf_op jit(solution)/shard_map/ppermute | solution.py:437
  99.6 2.5 collective-permute-start.25
  102.2 3.8 collective-permute-start.23
  106.0 6.1 %collective-permute-done.4.refs_4_ = bf16[64,1536]{1,0:T(8,128)(2,1)S(1)} collective-permute-done((bf16[64,1536]{1,0:T(8,128)(2,1)}, bf16[64,1536]{1,0:T(8,128)(2,1)S(1)}, u32[]{:S(2)}, u32[]{:S(2)}) %collective-permute-start.4) | collective-permute-done | bytes 196640 | tf_op jit(solution)/shard_map/ppermute | solution.py:437
  115.1 17.0 %collective-permute-done.25.refs_6_ = bf16[64,1536]{1,0:T(8,128)(2,1)S(1)} collective-permute-done((bf16[64,1536]{1,0:T(8,128)(2,1)S(1)}, bf16[64,1536]{1,0:T(8,128)(2,1)S(1)}, u32[]{:S(2)}, u32[]{:S(2)}) %collective-permute-start.25) | collective-permute-done | bytes 196640 | tf_op jit(solution)/shard_map/ppermute | solution.py:430
  132.3 3.8 collective-permute-start.8
  136.1 8.6 %collective-permute-done.22.refs_2_ = bf16[64,1536]{1,0:T(8,128)(2,1)S(1)} collective-permute-done((bf16[64,1536]{1,0:T(8,128)(2,1)}, bf16[64,1536]{1,0:T(8,128)(2,1)S(1)}, u32[]{:S(2)}, u32[]{:S(2)}) %collective-permute-start.22) | collective-permute-done | bytes 196640 | tf_op jit(solution)/shard_map/ppermute | solution.py:430
  145.4 12.4 %ffn.3 = (bf16[64,1536]{1,0:T(8,128)(2,1)}, bf16[64,1536]{1,0:T(8,128)(2,1)}, bf16[64,1536]{1,0:T(8,128)(2,1)}, bf16[64,1536]{1,0:T(8,128)(2,1)}, bf16[64,1536]{...) custom-call(bf16[64,1536]{1,0:T(8,128)(2,1)} %get-tuple-element.107., ...), custom_call_target="tpu_custom_call" | custom-call | flops 4831838208 | bytes 9437184 | tf_op jit(solution)/shard_map/ffn/pallas_call | solution.py:291
  157.9 3.3 collective-permute-start.39
  162.9 4.1 collective-permute-done.7.refs_2_
  168.3 12.4 %ffn.2 = (bf16[64,1536]{1,0:T(8,128)(2,1)}, bf16[64,1536]{1,0:T(8,128)(2,1)}, bf16[64,1536]{1,0:T(8,128)(2,1)}, bf16[64,1536]{1,0:T(8,128)(2,1)}, bf16[64,1536]{...) custom-call(bf16[64,1536]{1,0:T(8,128)(2,1)} %get-tuple-element.96.r, ...), custom_call_target="tpu_custom_call" | custom-call | flops 4831838208 | bytes 9437184 | tf_op jit(solution)/shard_map/ffn/pallas_call | solution.py:291
  182.1 6.2 %collective-permute-start.31 = (bf16[64,1536]{1,0:T(8,128)(2,1)}, bf16[64,1536]{1,0:T(8,128)(2,1)S(1)}, u32[]{:S(2)}, u32[]{:S(2)}) collective-permute-start(bf16[64,1536]{1,0:T(8,128)(2,1)} %get-tuple-element.114), channel_id=1, source_target_pairs={{0,2},{1,3},{2,0},{3,1},{4,6},{5,7},{6,4},{7,5},{8,10},{9,11},{10,... | collective-permute-start | bytes 589832 | tf_op jit(solution)/shard_map/ppermute | solution.py:437
  191.0 2.6 mid_back.3
  195.5 6.3 %collective-permute-start.42 = (bf16[64,1536]{1,0:T(8,128)(2,1)}, bf16[64,1536]{1,0:T(8,128)(2,1)S(1)}, u32[]{:S(2)}, u32[]{:S(2)}) collective-permute-start(bf16[64,1536]{1,0:T(8,128)(2,1)} %get-tuple-element.132.refs_0_), channel_id=1, source_target_pairs={{0,1},{1,2},{2,3},{3,0},{4,5},{5,6},{6,7},{7,4},{8,9},{9,10},{10,1... | collective-permute-start | bytes 589832 | tf_op jit(solution)/shard_map/ppermute | solution.py:430
  201.8 13.5 %collective-permute-done.31.refs_5_ = bf16[64,1536]{1,0:T(8,128)(2,1)S(1)} collective-permute-done((bf16[64,1536]{1,0:T(8,128)(2,1)}, bf16[64,1536]{1,0:T(8,128)(2,1)S(1)}, u32[]{:S(2)}, u32[]{:S(2)}) %collective-permute-start.31) | collective-permute-done | bytes 196640 | tf_op jit(solution)/shard_map/ppermute | solution.py:437
  216.1 2.6 mid_back.2
  218.7 2.5 collective-permute-start.33
  221.2 11.0 %collective-permute-done.43.refs_2_ = bf16[64,1536]{1,0:T(8,128)(2,1)S(1)} collective-permute-done((bf16[64,1536]{1,0:T(8,128)(2,1)}, bf16[64,1536]{1,0:T(8,128)(2,1)S(1)}, u32[]{:S(2)}, u32[]{:S(2)}) %collective-permute-start.43) | collective-permute-done | bytes 196640 | tf_op jit(solution)/shard_map/ppermute | solution.py:430
  233.0 14.4 %attn_bwd.3 = (bf16[64,1536]{1,0:T(8,128)(2,1)}, bf16[64,1536]{1,0:T(8,128)(2,1)}, bf16[64,1536]{1,0:T(8,128)(2,1)}, bf16[64,1536]{1,0:T(8,128)(2,1)}, bf16[256,...) custom-call(s32[1]{0:T(128)} %bitcast.1.me_ref, ...), custom_call_target="tpu_custom_call" | custom-call | flops 3355443200 | bytes 14629924 | tf_op jit(solution)/shard_map/attn_bwd/pallas_call | solution.py:38
  248.2 14.7 %attn_bwd.2 = (bf16[64,1536]{1,0:T(8,128)(2,1)}, bf16[64,1536]{1,0:T(8,128)(2,1)}, bf16[64,1536]{1,0:T(8,128)(2,1)}, bf16[64,1536]{1,0:T(8,128)(2,1)}, bf16[256,...) custom-call(s32[1]{0:T(128)} %bitcast.1.me_ref, ...), custom_call_target="tpu_custom_call" | custom-call | flops 3355443200 | bytes 14629924 | tf_op jit(solution)/shard_map/attn_bwd/pallas_call | solution.py:38
  263.0 3.2 convolution_convert_fusion
  267.1 2.5 pad_maximum_fusion.1
  269.6 6.7 %copy.90 = bf16[1536,1536]{1,0:T(8,128)(2,1)} copy(bf16[1536,1536]{0,1:T(8,128)(2,1)} %pad_maximum_fusion.1) | data formatting | bytes 9437184
  284.9 4.4 %pad_maximum_fusion = bf16[1536,3072]{0,1:T(8,128)(2,1)} fusion(bf16[1536,1024]{0,1:T(8,128)(2,1)S(1)} %convolution_convert_fusion.1, bf16[1536,1024]{0,1:T(8,128)(2,1)S(1)} %convolution_convert_fusion.2, bf16[1536,1024]{0,1:T(8,128)(2,1)S(1)} %convolution_convert_fusion.3), kind=kLoop, calls=%fused_computation | loop fusion | flops 28311552 | bytes 18874368 | tf_op jit(solution)/shard_map/concatenate | solution.py:526
  289.2 12.5 %copy.92 = bf16[1536,3072]{1,0:T(8,128)(2,1)} copy(bf16[1536,3072]{0,1:T(8,128)(2,1)} %pad_maximum_fusion) | data formatting | bytes 18874368
  308.1 3.9 collective-permute-done.27
  312.0 9.6 %collective-permute-done.28 = bf16[64,1536]{1,0:T(8,128)(2,1)S(1)} collective-permute-done((bf16[64,1536]{1,0:T(8,128)(2,1)S(1)}, bf16[64,1536]{1,0:T(8,128)(2,1)S(1)}, u32[]{:S(2)}, u32[]{:S(2)}) %collective-permute-start.28) | collective-permute-done | bytes 196640 | tf_op jit(solution)/shard_map/ppermute | solution.py:437
  323.2 2.8 collective-permute-done.49
  327.4 10.8 %collective-permute-done.13 = bf16[64,1536]{1,0:T(8,128)(2,1)S(1)} collective-permute-done((bf16[64,1536]{1,0:T(8,128)(2,1)S(1)}, bf16[64,1536]{1,0:T(8,128)(2,1)S(1)}, u32[]{:S(2)}, u32[]{:S(2)}) %collective-permute-start.13) | collective-permute-done | bytes 196640 | tf_op jit(solution)/shard_map/ppermute | solution.py:437
  340.1 3.4 collective-permute-start.45
  344.1 3.3 collective-permute-start.36
  349.1 2.5 slice.149
  352.3 12.4 %collective-permute-done.52 = f32[24,128]{1,0:T(8,128)S(1)} collective-permute-done((f32[24,128]{1,0:T(8,128)S(1)}, f32[24,128]{1,0:T(8,128)S(1)}, u32[]{:S(2)}, u32[]{:S(2)}) %collective-permute-start.52) | collective-permute-done | bytes 12320 | tf_op jit(solution)/shard_map/ppermute | solution.py:445
  364.8 4.5 %collective-permute-start.38 = (bf16[64,1536]{1,0:T(8,128)(2,1)S(1)}, bf16[64,1536]{1,0:T(8,128)(2,1)S(1)}, u32[]{:S(2)}, u32[]{:S(2)}) collective-permute-start(bf16[64,1536]{1,0:T(8,128)(2,1)S(1)} %copy-done.94), channel_id=1, source_target_pairs={{0,1},{1,2},{2,3},{3,0},{4,5},{5,6},{6,7},{7,4},{8,9},{9,10},{10,1... | collective-permute-start | bytes 589832 | tf_op jit(solution)/shard_map/ppermute | solution.py:437
  373.8 6.1 %collective-permute-done.37.refs_5_ = bf16[64,1536]{1,0:T(8,128)(2,1)S(1)} collective-permute-done((bf16[64,1536]{1,0:T(8,128)(2,1)S(1)}, bf16[64,1536]{1,0:T(8,128)(2,1)S(1)}, u32[]{:S(2)}, u32[]{:S(2)}) %collective-permute-start.37) | collective-permute-done | bytes 196640 | tf_op jit(solution)/shard_map/ppermute | solution.py:437
  388.9 19.6 %reduce-scatter.9.cloned.1.call-done = bf16[192,3072]{1,0:T(8,128)(2,1)} async-done(((bf16[1536,3072]{1,0:T(8,128)(2,1)}), bf16[192,3072]{1,0:T(8,128)(2,1)}) %reduce-scatter.9.cloned.1.call-update) | async-done | bytes 1179664
  413.2 2.4 copy.88
  (363 shorter events, 78.4 us)
Async XLA Ops:
  7.2 49.7 %all-gather.3.cloned.1.call-start = ((), (), s32[]{:S(2)}) async-start(), calls=%async_computation.2 | async-start | bytes 5750784 | tf_op jit(solution)/shard_map/all_gather | solution.py:482
  13.4 131.4 %all-gather.5.cloned.1.call-start = ((), (), s32[]{:S(2)}) async-start(), calls=%async_computation.3 | async-start | bytes 10616832 | tf_op jit(solution)/shard_map/all_gather | solution.py:483
  15.9 369.3 %reduce-scatter.7.cloned.1.call-start = ((), (), s32[]{:S(2)}) async-start(), calls=%async_computation.4 | async-start | bytes 5308416
  16.0 50.3 %collective-permute-start.2 = (bf16[64,1536]{1,0:T(8,128)(2,1)S(1)}, bf16[64,1536]{1,0:T(8,128)(2,1)S(1)}, u32[]{:S(2)}, u32[]{:S(2)}) collective-permute-start(bf16[64,1536]{1,0:T(8,128)(2,1)S(1)} %get-tuple-element.247.refs_0_), channel_id=1, source_target_pairs={{0,3},{1,0},{2,1},{3,2},{4,7},{5,4},{6,5},{7,6},{8,11},{9,8},{10,9... | collective-permute-start | bytes 589832 | tf_op jit(solution)/shard_map/ppermute | solution.py:430
  21.1 48.6 %collective-permute-start.1 = (bf16[64,1536]{1,0:T(8,128)(2,1)S(1)}, bf16[64,1536]{1,0:T(8,128)(2,1)S(1)}, u32[]{:S(2)}, u32[]{:S(2)}) collective-permute-start(bf16[64,1536]{1,0:T(8,128)(2,1)S(1)} %get-tuple-element.247.refs_0_), channel_id=1, source_target_pairs={{0,2},{1,3},{2,0},{3,1},{4,6},{5,7},{6,4},{7,5},{8,10},{9,11},{10,... | collective-permute-start | bytes 589832 | tf_op jit(solution)/shard_map/ppermute | solution.py:430
  21.1 16.1 %collective-permute-start.17 = (bf16[64,1536]{1,0:T(8,128)(2,1)S(1)}, bf16[64,1536]{1,0:T(8,128)(2,1)S(1)}, u32[]{:S(2)}, u32[]{:S(2)}) collective-permute-start(bf16[64,1536]{1,0:T(8,128)(2,1)S(1)} %get-tuple-element.248.refs_0_), channel_id=1, source_target_pairs={{0,3},{1,0},{2,1},{3,2},{4,7},{5,4},{6,5},{7,6},{8,11},{9,8},{10,9... | collective-permute-start | bytes 589832 | tf_op jit(solution)/shard_map/ppermute | solution.py:430
  21.6 33.5 %collective-permute-start.16 = (bf16[64,1536]{1,0:T(8,128)(2,1)S(1)}, bf16[64,1536]{1,0:T(8,128)(2,1)S(1)}, u32[]{:S(2)}, u32[]{:S(2)}) collective-permute-start(bf16[64,1536]{1,0:T(8,128)(2,1)S(1)} %get-tuple-element.248.refs_0_), channel_id=1, source_target_pairs={{0,2},{1,3},{2,0},{3,1},{4,6},{5,7},{6,4},{7,5},{8,10},{9,11},{10,... | collective-permute-start | bytes 589832 | tf_op jit(solution)/shard_map/ppermute | solution.py:430
  24.0 31.0 %collective-permute-start.15 = (bf16[64,1536]{1,0:T(8,128)(2,1)S(1)}, bf16[64,1536]{1,0:T(8,128)(2,1)S(1)}, u32[]{:S(2)}, u32[]{:S(2)}) collective-permute-start(bf16[64,1536]{1,0:T(8,128)(2,1)S(1)} %get-tuple-element.248.refs_0_), channel_id=1, source_target_pairs={{0,1},{1,2},{2,3},{3,0},{4,5},{5,6},{6,7},{7,4},{8,9},{9,10},{10,1... | collective-permute-start | bytes 589832 | tf_op jit(solution)/shard_map/ppermute | solution.py:430
  37.2 32.5 %collective-permute-start = (bf16[64,1536]{1,0:T(8,128)(2,1)S(1)}, bf16[64,1536]{1,0:T(8,128)(2,1)S(1)}, u32[]{:S(2)}, u32[]{:S(2)}) collective-permute-start(bf16[64,1536]{1,0:T(8,128)(2,1)S(1)} %get-tuple-element.247.refs_0_), channel_id=1, source_target_pairs={{0,1},{1,2},{2,3},{3,0},{4,5},{5,6},{6,7},{7,4},{8,9},{9,10},{10,1... | collective-permute-start | bytes 589832 | tf_op jit(solution)/shard_map/ppermute | solution.py:430
  55.0 44.6 %collective-permute-start.11 = (bf16[64,1536]{1,0:T(8,128)(2,1)S(1)}, bf16[64,1536]{1,0:T(8,128)(2,1)S(1)}, u32[]{:S(2)}, u32[]{:S(2)}) collective-permute-start(bf16[64,1536]{1,0:T(8,128)(2,1)S(1)} %get-tuple-element.245.refs_4_.refs_1_), channel_id=1, source_target_pairs={{0,3},{1,0},{2,1},{3,2},{4,7},{5,4},{6,5},{7,6},{8,11},{9,8},{10,9... | collective-permute-start | bytes 589832 | tf_op jit(solution)/shard_map/ppermute | solution.py:430
  55.0 47.1 %collective-permute-start.26 = (bf16[64,1536]{1,0:T(8,128)(2,1)S(1)}, bf16[64,1536]{1,0:T(8,128)(2,1)S(1)}, u32[]{:S(2)}, u32[]{:S(2)}) collective-permute-start(bf16[64,1536]{1,0:T(8,128)(2,1)S(1)} %get-tuple-element.246.refs_4_.refs_1_), channel_id=1, source_target_pairs={{0,3},{1,0},{2,1},{3,2},{4,7},{5,4},{6,5},{7,6},{8,11},{9,8},{10,9... | collective-permute-start | bytes 589832 | tf_op jit(solution)/shard_map/ppermute | solution.py:430
  69.7 18.5 %collective-permute-start.19 = (bf16[64,1536]{1,0:T(8,128)(2,1)}, bf16[64,1536]{1,0:T(8,128)(2,1)S(1)}, u32[]{:S(2)}, u32[]{:S(2)}) collective-permute-start(bf16[64,1536]{1,0:T(8,128)(2,1)} %get-tuple-element.104), channel_id=1, source_target_pairs={{0,2},{1,3},{2,0},{3,1},{4,6},{5,7},{6,4},{7,5},{8,10},{9,11},{10,... | collective-permute-start | bytes 589832 | tf_op jit(solution)/shard_map/ppermute | solution.py:437
  69.7 18.5 %collective-permute-start.20 = (bf16[64,1536]{1,0:T(8,128)(2,1)}, bf16[64,1536]{1,0:T(8,128)(2,1)S(1)}, u32[]{:S(2)}, u32[]{:S(2)}) collective-permute-start(bf16[64,1536]{1,0:T(8,128)(2,1)} %get-tuple-element.105), channel_id=1, source_target_pairs={{0,1},{1,2},{2,3},{3,0},{4,5},{5,6},{6,7},{7,4},{8,9},{9,10},{10,1... | collective-permute-start | bytes 589832 | tf_op jit(solution)/shard_map/ppermute | solution.py:437
  80.4 21.7 %collective-permute-start.3 = (bf16[64,1536]{1,0:T(8,128)(2,1)}, bf16[64,1536]{1,0:T(8,128)(2,1)S(1)}, u32[]{:S(2)}, u32[]{:S(2)}) collective-permute-start(bf16[64,1536]{1,0:T(8,128)(2,1)} %get-tuple-element.92), channel_id=1, source_target_pairs={{0,3},{1,0},{2,1},{3,2},{4,7},{5,4},{6,5},{7,6},{8,11},{9,8},{10,9... | collective-permute-start | bytes 589832 | tf_op jit(solution)/shard_map/ppermute | solution.py:437
  88.2 23.8 %collective-permute-start.4 = (bf16[64,1536]{1,0:T(8,128)(2,1)}, bf16[64,1536]{1,0:T(8,128)(2,1)S(1)}, u32[]{:S(2)}, u32[]{:S(2)}) collective-permute-start(bf16[64,1536]{1,0:T(8,128)(2,1)} %get-tuple-element.93), channel_id=1, source_target_pairs={{0,2},{1,3},{2,0},{3,1},{4,6},{5,7},{6,4},{7,5},{8,10},{9,11},{10,... | collective-permute-start | bytes 589832 | tf_op jit(solution)/shard_map/ppermute | solution.py:437
  88.2 23.8 %collective-permute-start.5 = (bf16[64,1536]{1,0:T(8,128)(2,1)}, bf16[64,1536]{1,0:T(8,128)(2,1)S(1)}, u32[]{:S(2)}, u32[]{:S(2)}) collective-permute-start(bf16[64,1536]{1,0:T(8,128)(2,1)} %get-tuple-element.94), channel_id=1, source_target_pairs={{0,1},{1,2},{2,3},{3,0},{4,5},{5,6},{6,7},{7,4},{8,9},{9,10},{10,1... | collective-permute-start | bytes 589832 | tf_op jit(solution)/shard_map/ppermute | solution.py:437
  99.6 32.6 %collective-permute-start.25 = (bf16[64,1536]{1,0:T(8,128)(2,1)S(1)}, bf16[64,1536]{1,0:T(8,128)(2,1)S(1)}, u32[]{:S(2)}, u32[]{:S(2)}) collective-permute-start(bf16[64,1536]{1,0:T(8,128)(2,1)S(1)} %get-tuple-element.246.refs_4_.refs_1_), channel_id=1, source_target_pairs={{0,2},{1,3},{2,0},{3,1},{4,6},{5,7},{6,4},{7,5},{8,10},{9,11},{10,... | collective-permute-start | bytes 589832 | tf_op jit(solution)/shard_map/ppermute | solution.py:430
  102.1 30.1 %collective-permute-start.24 = (bf16[64,1536]{1,0:T(8,128)(2,1)S(1)}, bf16[64,1536]{1,0:T(8,128)(2,1)S(1)}, u32[]{:S(2)}, u32[]{:S(2)}) collective-permute-start(bf16[64,1536]{1,0:T(8,128)(2,1)S(1)} %get-tuple-element.246.refs_4_.refs_1_), channel_id=1, source_target_pairs={{0,1},{1,2},{2,3},{3,0},{4,5},{5,6},{6,7},{7,4},{8,9},{9,10},{10,1... | collective-permute-start | bytes 589832 | tf_op jit(solution)/shard_map/ppermute | solution.py:430
  102.2 30.1 %collective-permute-start.23 = (bf16[64,1536]{1,0:T(8,128)(2,1)}, bf16[64,1536]{1,0:T(8,128)(2,1)S(1)}, u32[]{:S(2)}, u32[]{:S(2)}) collective-permute-start(bf16[64,1536]{1,0:T(8,128)(2,1)} %get-tuple-element.107.refs_0_), channel_id=1, source_target_pairs={{0,3},{1,0},{2,1},{3,2},{4,7},{5,4},{6,5},{7,6},{8,11},{9,8},{10,9... | collective-permute-start | bytes 589832 | tf_op jit(solution)/shard_map/ppermute | solution.py:430
  112.0 32.7 %collective-permute-start.22 = (bf16[64,1536]{1,0:T(8,128)(2,1)}, bf16[64,1536]{1,0:T(8,128)(2,1)S(1)}, u32[]{:S(2)}, u32[]{:S(2)}) collective-permute-start(bf16[64,1536]{1,0:T(8,128)(2,1)} %get-tuple-element.107.refs_0_), channel_id=1, source_target_pairs={{0,2},{1,3},{2,0},{3,1},{4,6},{5,7},{6,4},{7,5},{8,10},{9,11},{10,... | collective-permute-start | bytes 589832 | tf_op jit(solution)/shard_map/ppermute | solution.py:430
  112.1 32.6 %collective-permute-start.21 = (bf16[64,1536]{1,0:T(8,128)(2,1)}, bf16[64,1536]{1,0:T(8,128)(2,1)S(1)}, u32[]{:S(2)}, u32[]{:S(2)}) collective-permute-start(bf16[64,1536]{1,0:T(8,128)(2,1)} %get-tuple-element.107.refs_0_), channel_id=1, source_target_pairs={{0,1},{1,2},{2,3},{3,0},{4,5},{5,6},{6,7},{7,4},{8,9},{9,10},{10,1... | collective-permute-start | bytes 589832 | tf_op jit(solution)/shard_map/ppermute | solution.py:430
  132.2 25.7 %collective-permute-start.10 = (bf16[64,1536]{1,0:T(8,128)(2,1)S(1)}, bf16[64,1536]{1,0:T(8,128)(2,1)S(1)}, u32[]{:S(2)}, u32[]{:S(2)}) collective-permute-start(bf16[64,1536]{1,0:T(8,128)(2,1)S(1)} %get-tuple-element.245.refs_4_.refs_1_), channel_id=1, source_target_pairs={{0,2},{1,3},{2,0},{3,1},{4,6},{5,7},{6,4},{7,5},{8,10},{9,11},{10,... | collective-permute-start | bytes 589832 | tf_op jit(solution)/shard_map/ppermute | solution.py:430
  132.2 29.0 %collective-permute-start.9 = (bf16[64,1536]{1,0:T(8,128)(2,1)S(1)}, bf16[64,1536]{1,0:T(8,128)(2,1)S(1)}, u32[]{:S(2)}, u32[]{:S(2)}) collective-permute-start(bf16[64,1536]{1,0:T(8,128)(2,1)S(1)} %get-tuple-element.245.refs_4_.refs_1_), channel_id=1, source_target_pairs={{0,1},{1,2},{2,3},{3,0},{4,5},{5,6},{6,7},{7,4},{8,9},{9,10},{10,1... | collective-permute-start | bytes 589832 | tf_op jit(solution)/shard_map/ppermute | solution.py:430
  132.3 30.0 %collective-permute-start.8 = (bf16[64,1536]{1,0:T(8,128)(2,1)}, bf16[64,1536]{1,0:T(8,128)(2,1)S(1)}, u32[]{:S(2)}, u32[]{:S(2)}) collective-permute-start(bf16[64,1536]{1,0:T(8,128)(2,1)} %get-tuple-element.96.refs_0_), channel_id=1, source_target_pairs={{0,3},{1,0},{2,1},{3,2},{4,7},{5,4},{6,5},{7,6},{8,11},{9,8},{10,9... | collective-permute-start | bytes 589832 | tf_op jit(solution)/shard_map/ppermute | solution.py:430
  144.7 22.3 %collective-permute-start.7 = (bf16[64,1536]{1,0:T(8,128)(2,1)}, bf16[64,1536]{1,0:T(8,128)(2,1)S(1)}, u32[]{:S(2)}, u32[]{:S(2)}) collective-permute-start(bf16[64,1536]{1,0:T(8,128)(2,1)} %get-tuple-element.96.refs_0_), channel_id=1, source_target_pairs={{0,2},{1,3},{2,0},{3,1},{4,6},{5,7},{6,4},{7,5},{8,10},{9,11},{10,... | collective-permute-start | bytes 589832 | tf_op jit(solution)/shard_map/ppermute | solution.py:430
  144.7 22.3 %collective-permute-start.6 = (bf16[64,1536]{1,0:T(8,128)(2,1)}, bf16[64,1536]{1,0:T(8,128)(2,1)S(1)}, u32[]{:S(2)}, u32[]{:S(2)}) collective-permute-start(bf16[64,1536]{1,0:T(8,128)(2,1)} %get-tuple-element.96.refs_0_), channel_id=1, source_target_pairs={{0,1},{1,2},{2,3},{3,0},{4,5},{5,6},{6,7},{7,4},{8,9},{9,10},{10,1... | collective-permute-start | bytes 589832 | tf_op jit(solution)/shard_map/ppermute | solution.py:430
  157.9 30.4 %collective-permute-start.39 = (bf16[64,1536]{1,0:T(8,128)(2,1)}, bf16[64,1536]{1,0:T(8,128)(2,1)S(1)}, u32[]{:S(2)}, u32[]{:S(2)}) collective-permute-start(bf16[64,1536]{1,0:T(8,128)(2,1)} %get-tuple-element.128), channel_id=1, source_target_pairs={{0,3},{1,0},{2,1},{3,2},{4,7},{5,4},{6,5},{7,6},{8,11},{9,8},{10,9... | collective-permute-start | bytes 589832 | tf_op jit(solution)/shard_map/ppermute | solution.py:437
  161.2 29.1 %collective-permute-start.40 = (bf16[64,1536]{1,0:T(8,128)(2,1)}, bf16[64,1536]{1,0:T(8,128)(2,1)S(1)}, u32[]{:S(2)}, u32[]{:S(2)}) collective-permute-start(bf16[64,1536]{1,0:T(8,128)(2,1)} %get-tuple-element.129), channel_id=1, source_target_pairs={{0,2},{1,3},{2,0},{3,1},{4,6},{5,7},{6,4},{7,5},{8,10},{9,11},{10,... | collective-permute-start | bytes 589832 | tf_op jit(solution)/shard_map/ppermute | solution.py:437
  162.3 28.0 %collective-permute-start.41 = (bf16[64,1536]{1,0:T(8,128)(2,1)}, bf16[64,1536]{1,0:T(8,128)(2,1)S(1)}, u32[]{:S(2)}, u32[]{:S(2)}) collective-permute-start(bf16[64,1536]{1,0:T(8,128)(2,1)} %get-tuple-element.130), channel_id=1, source_target_pairs={{0,1},{1,2},{2,3},{3,0},{4,5},{5,6},{6,7},{7,4},{8,9},{9,10},{10,1... | collective-permute-start | bytes 589832 | tf_op jit(solution)/shard_map/ppermute | solution.py:437
  182.1 33.2 %collective-permute-start.31 = (bf16[64,1536]{1,0:T(8,128)(2,1)}, bf16[64,1536]{1,0:T(8,128)(2,1)S(1)}, u32[]{:S(2)}, u32[]{:S(2)}) collective-permute-start(bf16[64,1536]{1,0:T(8,128)(2,1)} %get-tuple-element.114), channel_id=1, source_target_pairs={{0,2},{1,3},{2,0},{3,1},{4,6},{5,7},{6,4},{7,5},{8,10},{9,11},{10,... | collective-permute-start | bytes 589832 | tf_op jit(solution)/shard_map/ppermute | solution.py:437
  188.3 27.0 %collective-permute-start.32 = (bf16[64,1536]{1,0:T(8,128)(2,1)}, bf16[64,1536]{1,0:T(8,128)(2,1)S(1)}, u32[]{:S(2)}, u32[]{:S(2)}) collective-permute-start(bf16[64,1536]{1,0:T(8,128)(2,1)} %get-tuple-element.115), channel_id=1, source_target_pairs={{0,1},{1,2},{2,3},{3,0},{4,5},{5,6},{6,7},{7,4},{8,9},{9,10},{10,1... | collective-permute-start | bytes 589832 | tf_op jit(solution)/shard_map/ppermute | solution.py:437
  193.6 25.1 %collective-permute-start.44 = (bf16[64,1536]{1,0:T(8,128)(2,1)}, bf16[64,1536]{1,0:T(8,128)(2,1)S(1)}, u32[]{:S(2)}, u32[]{:S(2)}) collective-permute-start(bf16[64,1536]{1,0:T(8,128)(2,1)} %get-tuple-element.132.refs_0_), channel_id=1, source_target_pairs={{0,3},{1,0},{2,1},{3,2},{4,7},{5,4},{6,5},{7,6},{8,11},{9,8},{10,9... | collective-permute-start | bytes 589832 | tf_op jit(solution)/shard_map/ppermute | solution.py:430
  195.5 36.7 %collective-permute-start.43 = (bf16[64,1536]{1,0:T(8,128)(2,1)}, bf16[64,1536]{1,0:T(8,128)(2,1)S(1)}, u32[]{:S(2)}, u32[]{:S(2)}) collective-permute-start(bf16[64,1536]{1,0:T(8,128)(2,1)} %get-tuple-element.132.refs_0_), channel_id=1, source_target_pairs={{0,2},{1,3},{2,0},{3,1},{4,6},{5,7},{6,4},{7,5},{8,10},{9,11},{10,... | collective-permute-start | bytes 589832 | tf_op jit(solution)/shard_map/ppermute | solution.py:430
  195.5 36.7 %collective-permute-start.42 = (bf16[64,1536]{1,0:T(8,128)(2,1)}, bf16[64,1536]{1,0:T(8,128)(2,1)S(1)}, u32[]{:S(2)}, u32[]{:S(2)}) collective-permute-start(bf16[64,1536]{1,0:T(8,128)(2,1)} %get-tuple-element.132.refs_0_), channel_id=1, source_target_pairs={{0,1},{1,2},{2,3},{3,0},{4,5},{5,6},{6,7},{7,4},{8,9},{9,10},{10,1... | collective-permute-start | bytes 589832 | tf_op jit(solution)/shard_map/ppermute | solution.py:430
  218.7 28.7 %collective-permute-start.35 = (bf16[64,1536]{1,0:T(8,128)(2,1)}, bf16[64,1536]{1,0:T(8,128)(2,1)S(1)}, u32[]{:S(2)}, u32[]{:S(2)}) collective-permute-start(bf16[64,1536]{1,0:T(8,128)(2,1)} %get-tuple-element.117.refs_0_), channel_id=1, source_target_pairs={{0,3},{1,0},{2,1},{3,2},{4,7},{5,4},{6,5},{7,6},{8,11},{9,8},{10,9... | collective-permute-start | bytes 589832 | tf_op jit(solution)/shard_map/ppermute | solution.py:430
  218.7 28.7 %collective-permute-start.34 = (bf16[64,1536]{1,0:T(8,128)(2,1)}, bf16[64,1536]{1,0:T(8,128)(2,1)S(1)}, u32[]{:S(2)}, u32[]{:S(2)}) collective-permute-start(bf16[64,1536]{1,0:T(8,128)(2,1)} %get-tuple-element.117.refs_0_), channel_id=1, source_target_pairs={{0,2},{1,3},{2,0},{3,1},{4,6},{5,7},{6,4},{7,5},{8,10},{9,11},{10,... | collective-permute-start | bytes 589832 | tf_op jit(solution)/shard_map/ppermute | solution.py:430
  218.7 28.7 %collective-permute-start.33 = (bf16[64,1536]{1,0:T(8,128)(2,1)}, bf16[64,1536]{1,0:T(8,128)(2,1)S(1)}, u32[]{:S(2)}, u32[]{:S(2)}) collective-permute-start(bf16[64,1536]{1,0:T(8,128)(2,1)} %get-tuple-element.117.refs_0_), channel_id=1, source_target_pairs={{0,1},{1,2},{2,3},{3,0},{4,5},{5,6},{6,7},{7,4},{8,9},{9,10},{10,1... | collective-permute-start | bytes 589832 | tf_op jit(solution)/shard_map/ppermute | solution.py:430
  276.4 132.2 %reduce-scatter.9.cloned.1.call-start = ((), (), s32[]{:S(2)}) async-start(), calls=%async_computation.5 | async-start | bytes 10616832
  303.0 18.6 %collective-permute-start.28 = (bf16[64,1536]{1,0:T(8,128)(2,1)S(1)}, bf16[64,1536]{1,0:T(8,128)(2,1)S(1)}, u32[]{:S(2)}, u32[]{:S(2)}) collective-permute-start(bf16[64,1536]{1,0:T(8,128)(2,1)S(1)} %copy-done.86), channel_id=1, source_target_pairs={{0,2},{1,3},{2,0},{3,1},{4,6},{5,7},{6,4},{7,5},{8,10},{9,11},{10,... | collective-permute-start | bytes 589832 | tf_op jit(solution)/shard_map/ppermute | solution.py:437
  303.2 19.8 %collective-permute-start.29 = (bf16[64,1536]{1,0:T(8,128)(2,1)S(1)}, bf16[64,1536]{1,0:T(8,128)(2,1)S(1)}, u32[]{:S(2)}, u32[]{:S(2)}) collective-permute-start(bf16[64,1536]{1,0:T(8,128)(2,1)S(1)} %copy-done.85), channel_id=1, source_target_pairs={{0,1},{1,2},{2,3},{3,0},{4,5},{5,6},{6,7},{7,4},{8,9},{9,10},{10,1... | collective-permute-start | bytes 589832 | tf_op jit(solution)/shard_map/ppermute | solution.py:437
  305.2 22.2 %collective-permute-start.12 = (bf16[64,1536]{1,0:T(8,128)(2,1)S(1)}, bf16[64,1536]{1,0:T(8,128)(2,1)S(1)}, u32[]{:S(2)}, u32[]{:S(2)}) collective-permute-start(bf16[64,1536]{1,0:T(8,128)(2,1)S(1)} %copy-done.91), channel_id=1, source_target_pairs={{0,3},{1,0},{2,1},{3,2},{4,7},{5,4},{6,5},{7,6},{8,11},{9,8},{10,9... | collective-permute-start | bytes 589832 | tf_op jit(solution)/shard_map/ppermute | solution.py:437
  307.5 30.7 %collective-permute-start.13 = (bf16[64,1536]{1,0:T(8,128)(2,1)S(1)}, bf16[64,1536]{1,0:T(8,128)(2,1)S(1)}, u32[]{:S(2)}, u32[]{:S(2)}) collective-permute-start(bf16[64,1536]{1,0:T(8,128)(2,1)S(1)} %copy-done.90), channel_id=1, source_target_pairs={{0,2},{1,3},{2,0},{3,1},{4,6},{5,7},{6,4},{7,5},{8,10},{9,11},{10,... | collective-permute-start | bytes 589832 | tf_op jit(solution)/shard_map/ppermute | solution.py:437
  312.0 26.2 %collective-permute-start.14 = (bf16[64,1536]{1,0:T(8,128)(2,1)S(1)}, bf16[64,1536]{1,0:T(8,128)(2,1)S(1)}, u32[]{:S(2)}, u32[]{:S(2)}) collective-permute-start(bf16[64,1536]{1,0:T(8,128)(2,1)S(1)} %copy-done.89), channel_id=1, source_target_pairs={{0,1},{1,2},{2,3},{3,0},{4,5},{5,6},{6,7},{7,4},{8,9},{9,10},{10,1... | collective-permute-start | bytes 589832 | tf_op jit(solution)/shard_map/ppermute | solution.py:437
  340.1 24.6 %collective-permute-start.45 = (bf16[64,1536]{1,0:T(8,128)(2,1)}, bf16[64,1536]{1,0:T(8,128)(2,1)S(1)}, u32[]{:S(2)}, u32[]{:S(2)}) collective-permute-start(bf16[64,1536]{1,0:T(8,128)(2,1)} %get-tuple-element.139), channel_id=1, source_target_pairs={{0,3},{1,0},{2,1},{3,2},{4,7},{5,4},{6,5},{7,6},{8,11},{9,8},{10,9... | collective-permute-start | bytes 589832 | tf_op jit(solution)/shard_map/ppermute | solution.py:437
  343.5 27.2 %collective-permute-start.46 = (bf16[64,1536]{1,0:T(8,128)(2,1)S(1)}, bf16[64,1536]{1,0:T(8,128)(2,1)S(1)}, u32[]{:S(2)}, u32[]{:S(2)}) collective-permute-start(bf16[64,1536]{1,0:T(8,128)(2,1)S(1)} %copy-done.93), channel_id=1, source_target_pairs={{0,2},{1,3},{2,0},{3,1},{4,6},{5,7},{6,4},{7,5},{8,10},{9,11},{10,... | collective-permute-start | bytes 589832 | tf_op jit(solution)/shard_map/ppermute | solution.py:437
  343.5 27.2 %collective-permute-start.47 = (bf16[64,1536]{1,0:T(8,128)(2,1)S(1)}, bf16[64,1536]{1,0:T(8,128)(2,1)S(1)}, u32[]{:S(2)}, u32[]{:S(2)}) collective-permute-start(bf16[64,1536]{1,0:T(8,128)(2,1)S(1)} %copy-done.92), channel_id=1, source_target_pairs={{0,1},{1,2},{2,3},{3,0},{4,5},{5,6},{6,7},{7,4},{8,9},{9,10},{10,1... | collective-permute-start | bytes 589832 | tf_op jit(solution)/shard_map/ppermute | solution.py:437
  344.1 29.7 %collective-permute-start.36 = (bf16[64,1536]{1,0:T(8,128)(2,1)S(1)}, bf16[64,1536]{1,0:T(8,128)(2,1)S(1)}, u32[]{:S(2)}, u32[]{:S(2)}) collective-permute-start(bf16[64,1536]{1,0:T(8,128)(2,1)S(1)} %copy-done.96), channel_id=1, source_target_pairs={{0,3},{1,0},{2,1},{3,2},{4,7},{5,4},{6,5},{7,6},{8,11},{9,8},{10,9... | collective-permute-start | bytes 589832 | tf_op jit(solution)/shard_map/ppermute | solution.py:437
  347.4 17.4 %collective-permute-start.52 = (f32[24,128]{1,0:T(8,128)S(1)}, f32[24,128]{1,0:T(8,128)S(1)}, u32[]{:S(2)}, u32[]{:S(2)}) collective-permute-start(f32[24,128]{1,0:T(8,128)S(1)} %get-tuple-element.250), channel_id=1, source_target_pairs={{0,2},{1,3},{2,0},{3,1},{4,6},{5,7},{6,4},{7,5},{8,10},{9,11},{10,... | collective-permute-start | bytes 36872 | tf_op jit(solution)/shard_map/ppermute | solution.py:445
  (106 other events, 1168.5 us)
Sparse Core Ops, SparseCore 0:
  13.5 43.2 all-gather.2
  58.7 58.8 all-gather.4
  276.5 51.6 reduce-scatter.6
  331.9 76.5 reduce-scatter.8
